TPU v7x, 128 devices: a whole 4x4x4 slice. The times are simulated.
128 devices in a mesh: ctx: 8 (over x, y_hi), head: 16 (over z, y_lo, core).
Axes of the slice: x: 4, y: 4 (y_hi: 2, y_lo: 2; y = y_hi * 2 + y_lo), z: 4, core: 2. Of those that a mesh axis runs over, the one named last changes fastest.
Arguments:
- query: bfloat16 [131072, 1024], P(('ctx', 'head')), may hold values from -7 to 7
- key: bfloat16 [131072, 1024], P(('ctx', 'head')), may hold values from -7 to 7
- value: bfloat16 [131072, 1024], P(('ctx', 'head')), may hold values from -6 to 6
- pattern: int32 [16, 1024, 12], P('head', 'ctx'), may hold values from 0 to 1023, as said below
Outputs:
- attended: bfloat16 [131072, 1024], P(('ctx', 'head'))
Inputs may be any that keep to these rules, and one draw needn't show every extreme that they name: pattern[h, b] holds 12 different key block numbers, the first of them b itself. Cut the blocks into aligned groups of 128; for each head and each group, the key blocks read by the group's query blocks that lie outside the group are exactly 2 different blocks from each other group.
All inputs are finite; a program needn't handle non-finite values.
Results may differ from a plain program's by a relative error of at most 0.0047.
Values may be sent and summed in bfloat16 or wider, within the bound.
No kernel may reach another device: no remote copies, remote signals or barrier semaphores. Data moves between devices by JAX's collectives and lax.ppermute only.
A program may use at most 192 MiB of HBM per device.

v0:
```python
import math

import jax
import jax.numpy as jnp
from jax import lax
from jax.sharding import PartitionSpec as P

DH = 64
BLK = 128
KPER = 12
PMOST = 2


def on_device(query, key, value, pattern):
    q_loc, k_loc, v_loc = (
        lax.all_to_all(query, "head", split_axis=1, concat_axis=0, tiled=True),
        lax.all_to_all(key, "head", split_axis=1, concat_axis=0, tiled=True),
        lax.all_to_all(value, "head", split_axis=1, concat_axis=0, tiled=True),
    )
    tok_rows = q_loc.shape[0]
    feat_width = q_loc.shape[1]
    nheads = feat_width // DH
    query_count = tok_rows // BLK
    ranges = lax.axis_size("ctx")
    own_range = lax.axis_index("ctx")
    all_blocks = query_count * ranges
    positions = jnp.arange(query_count, dtype=jnp.int32)
    block_ids = jnp.arange(all_blocks, dtype=jnp.int32)
    head_grid = jnp.arange(nheads, dtype=jnp.int32)[None, :, None]
    score_scale = DH ** (-0.5)
    head_idx = 0
    rows_pat = pattern[head_idx]
    outside = rows_pat // query_count != own_range
    matches = jnp.logical_and(rows_pat[:, :, None] == block_ids, outside[:, :, None])
    present = jnp.any(matches, axis=(0, 1)).astype(jnp.int32).reshape(ranges, query_count)
    ranking = present * (2 * query_count) + (query_count - 1 - positions)
    wanted_list = [lax.top_k(ranking, PMOST)[1]]
    wanted = jnp.stack(wanted_list, axis=1)
    kv_parts = []
    kv_parts.append(k_loc)
    kv_parts.append(v_loc)
    kv_pack = jnp.concatenate(kv_parts, axis=1)
    kv_blocks = kv_pack.reshape(query_count, BLK, nheads, 2 * DH)
    blank_table = jnp.zeros((ranges, nheads, PMOST, BLK, 2 * DH), jnp.bfloat16)
    wanted_global = jnp.arange(ranges, dtype=jnp.int32)[:, None, None] * query_count + wanted
    piece = lax.all_gather(kv_pack, "ctx", axis=0, tiled=True)
    piece_count = piece.shape[0] // BLK
    piece_blocks = piece.reshape(piece_count, BLK, nheads, 2 * DH)
    inside = jnp.logical_and(wanted_global >= 0, wanted_global < piece_count)
    picked = piece_blocks[jnp.clip(wanted_global, 0, piece_count - 1), :, head_grid, :]
    remote_table = jnp.where(inside[..., None, None], picked, blank_table)
    group_size = math.gcd(query_count, 16)
    ngroups = query_count // group_size
    slot_ids = jnp.arange(PMOST, dtype=jnp.int32)
    head_idx = 0
    kv_table = jnp.concatenate(
        [
            kv_blocks[:, :, head_idx, :],
            remote_table[:, head_idx].reshape(ranges * PMOST, BLK, 2 * DH),
        ],
        axis=0,
    )
    rows_pat = pattern[head_idx]
    owner_range = rows_pat // query_count
    local_pos = rows_pat % query_count
    found = wanted[:, head_idx][owner_range] == local_pos[..., None]
    slot_index = jnp.sum(jnp.where(found, slot_ids, 0), axis=-1)
    table_index = jnp.where(
        owner_range == own_range, local_pos, query_count + owner_range * PMOST + slot_index
    )
    q_groups = q_loc.reshape(ngroups, group_size, BLK, DH)
    idx_groups = table_index.reshape(ngroups, group_size, KPER)

    def attend(inputs, kv_table=kv_table):
        q_grp, idx_grp = inputs
        picked = kv_table[idx_grp]
        scores = (
            jnp.einsum(
                "gqd,gjkd->gqjk", q_grp, picked[..., :DH], preferred_element_type=jnp.float32
            )
            * score_scale
        )
        row_top = jnp.max(scores, axis=(2, 3))
        exp_scores = jnp.exp(scores - row_top[:, :, None, None])
        row_total = jnp.sum(exp_scores, axis=(2, 3))
        summed = jnp.einsum(
            "gqjk,gjkd->gqd",
            exp_scores.astype(jnp.bfloat16),
            picked[..., DH:],
            preferred_element_type=jnp.float32,
        )
        return (summed / row_total[..., None]).astype(jnp.bfloat16)

    head_outputs = lax.map(attend, (q_groups, idx_groups)).reshape(tok_rows, DH)
    return lax.all_to_all(head_outputs, "head", split_axis=0, concat_axis=1, tiled=True)


def solution(mesh):
    placed = (
        P(("ctx", "head"), None),
        P(("ctx", "head"), None),
        P(("ctx", "head"), None),
        P("head", "ctx", None),
    )
    return jax.shard_map(
        on_device, mesh=mesh, in_specs=placed, out_specs=P(("ctx", "head"), None), check_vma=False
    )
```

profile of v0, /device:TPU:1, one launch (start us, length us, event | category | flops | bytes accessed | tf_op | source)
XLA Modules:
  0.0 788.5 jit_solution(6231008476632309845)
XLA Ops:
  7.4 3.9 copy.142
  11.3 7.8 all-to-all-start.1
  19.2 3.9 copy.144
  23.1 23.2 %all-to-all-done.1 = bf16[1024,16,64]{0,2,1:T(8,128)(2,1)S(1)} async-done(((bf16[1024,16,64]{0,2,1:T(8,128)(2,1)}), bf16[1024,16,64]{0,2,1:T(8,128)(2,1)S(1)}, u32[]{:S(2)}, u32[]{:S(2)}) %all-to-all-start.1) | async-done | bytes 2097184 | tf_op jit(solution)/shard_map/all_to_all | solution.py:17
  46.3 5.0 all-to-all-start.2
  55.4 23.2 %all-to-all-done.2 = bf16[1024,16,64]{0,2,1:T(8,128)(2,1)} async-done(((bf16[1024,16,64]{0,2,1:T(8,128)(2,1)}), bf16[1024,16,64]{0,2,1:T(8,128)(2,1)}, u32[]{:S(2)}, u32[]{:S(2)}) %all-to-all-start.2) | async-done | bytes 2097184 | tf_op jit(solution)/shard_map/all_to_all | solution.py:18
  80.8 2.4 pad_maximum_fusion.1
  83.3 4.0 copy.136
  87.3 5.0 all-to-all-start
  94.7 2.6 gather_fusion.1
  97.8 2.5 copy.143
  100.3 4.3 concatenate.16
  104.6 2.7 copy.145
  107.3 2.3 concatenate.17
  109.6 26.3 %all-to-all-done = bf16[1024,16,64]{0,2,1:T(8,128)(2,1)} async-done(((bf16[1024,16,64]{0,2,1:T(8,128)(2,1)}), bf16[1024,16,64]{0,2,1:T(8,128)(2,1)}, u32[]{:S(2)}, u32[]{:S(2)}) %all-to-all-start) | async-done | bytes 2097184 | tf_op jit(solution)/shard_map/all_to_all | solution.py:16
  135.9 2.7 copy.137
  138.7 2.3 reshape.204
  141.0 299.3 %all-gather.2.cloned.1.call-done = bf16[131072,128]{0,1:T(8,128)(2,1)} async-done(((bf16[16384,128]{0,1:T(8,128)(2,1)}), bf16[131072,128]{0,1:T(8,128)(2,1)}) %all-gather.2.cloned.1.call-update) | async-done | bytes 33554448 | tf_op jit(solution)/shard_map/all_gather | solution.py:46
  440.2 44.0 %copy.148 = bf16[131072,128]{1,0:T(8,128)(2,1)} copy(bf16[131072,128]{0,1:T(8,128)(2,1)} %all-gather.2.cloned.1.call-done) | data formatting | bytes 67108864 | tf_op jit(solution)/shard_map/all_gather | solution.py:46
  486.4 5.0 pad_maximum_fusion
  491.4 7.1 copy.156
  498.4 243.9 %while.10 = (s32[]{:T(128)}, bf16[8,16,128,64]{2,1,0,3:T(8,128)(2,1)}, bf16[8,16,128,64]{2,1,0,3:T(8,128)(2,1)}, s32[8,16,12]{2,1,0:T(8,128)S(1)}, bf16[144,128,128]{2,1,0:T(8,128)(2,1)}, /*index=5*/s32[]{:T(128)}) while((s32[]{:T(128)}, bf16[8,16,128,64]{2,1,0,3:T(8,128)(2,1)}, bf16[8,16,128,64]{2,1,0,3:T(8,128)(2,1)}, ...), condition=%wide.region_6.7_spmd, body=%wide.region_3.6_spmd.sunk | while | flops 830731840 | bytes 89703544 | solution.py:94
  498.5 10.4 %gather_fusion = bf16[192,128,128]{2,1,0:T(8,128)(2,1)} fusion(bf16[144,128,128]{2,1,0:T(8,128)(2,1)} %get-tuple-element.132, s32[1024]{0:T(1024)S(1)} %pad_clamp_fusion.3), kind=kCustom, calls=%fused_computation.clone.1 | custom fusion | bytes 12583680 | tf_op jit(solution)/shard_map/while/body/eval_jaxpr/gather | solution.py:76
  508.9 8.6 %copy.187 = bf16[192,128,128]{1,2,0:T(8,128)(2,1)} copy(bf16[192,128,128]{2,1,0:T(8,128)(2,1)} %gather_fusion) | data formatting | bytes 12582912 | tf_op jit(solution)/shard_map/while/body/eval_jaxpr/gather | solution.py:76
  518.7 4.4 multiply_reduce_fusion.2
  523.1 2.0 fusion.46
  525.1 2.9 fusion.47
  529.0 10.4 %gather_fusion = bf16[192,128,128]{2,1,0:T(8,128)(2,1)} fusion(bf16[144,128,128]{2,1,0:T(8,128)(2,1)} %get-tuple-element.132, s32[1024]{0:T(1024)S(1)} %pad_clamp_fusion.3), kind=kCustom, calls=%fused_computation.clone.1 | custom fusion | bytes 12583680 | tf_op jit(solution)/shard_map/while/body/eval_jaxpr/gather | solution.py:76
  539.4 8.6 %copy.187 = bf16[192,128,128]{1,2,0:T(8,128)(2,1)} copy(bf16[192,128,128]{2,1,0:T(8,128)(2,1)} %gather_fusion) | data formatting | bytes 12582912 | tf_op jit(solution)/shard_map/while/body/eval_jaxpr/gather | solution.py:76
  549.2 4.4 multiply_reduce_fusion.2
  553.5 2.0 fusion.46
  555.6 2.9 fusion.47
  559.5 10.4 %gather_fusion = bf16[192,128,128]{2,1,0:T(8,128)(2,1)} fusion(bf16[144,128,128]{2,1,0:T(8,128)(2,1)} %get-tuple-element.132, s32[1024]{0:T(1024)S(1)} %pad_clamp_fusion.3), kind=kCustom, calls=%fused_computation.clone.1 | custom fusion | bytes 12583680 | tf_op jit(solution)/shard_map/while/body/eval_jaxpr/gather | solution.py:76
  569.9 8.6 %copy.187 = bf16[192,128,128]{1,2,0:T(8,128)(2,1)} copy(bf16[192,128,128]{2,1,0:T(8,128)(2,1)} %gather_fusion) | data formatting | bytes 12582912 | tf_op jit(solution)/shard_map/while/body/eval_jaxpr/gather | solution.py:76
  579.7 4.4 multiply_reduce_fusion.2
  584.0 2.0 fusion.46
  586.1 2.9 fusion.47
  590.0 10.4 %gather_fusion = bf16[192,128,128]{2,1,0:T(8,128)(2,1)} fusion(bf16[144,128,128]{2,1,0:T(8,128)(2,1)} %get-tuple-element.132, s32[1024]{0:T(1024)S(1)} %pad_clamp_fusion.3), kind=kCustom, calls=%fused_computation.clone.1 | custom fusion | bytes 12583680 | tf_op jit(solution)/shard_map/while/body/eval_jaxpr/gather | solution.py:76
  600.4 8.6 %copy.187 = bf16[192,128,128]{1,2,0:T(8,128)(2,1)} copy(bf16[192,128,128]{2,1,0:T(8,128)(2,1)} %gather_fusion) | data formatting | bytes 12582912 | tf_op jit(solution)/shard_map/while/body/eval_jaxpr/gather | solution.py:76
  610.2 4.4 multiply_reduce_fusion.2
  614.5 2.0 fusion.46
  616.6 2.9 fusion.47
  620.5 10.4 %gather_fusion = bf16[192,128,128]{2,1,0:T(8,128)(2,1)} fusion(bf16[144,128,128]{2,1,0:T(8,128)(2,1)} %get-tuple-element.132, s32[1024]{0:T(1024)S(1)} %pad_clamp_fusion.3), kind=kCustom, calls=%fused_computation.clone.1 | custom fusion | bytes 12583680 | tf_op jit(solution)/shard_map/while/body/eval_jaxpr/gather | solution.py:76
  630.9 8.6 %copy.187 = bf16[192,128,128]{1,2,0:T(8,128)(2,1)} copy(bf16[192,128,128]{2,1,0:T(8,128)(2,1)} %gather_fusion) | data formatting | bytes 12582912 | tf_op jit(solution)/shard_map/while/body/eval_jaxpr/gather | solution.py:76
  640.7 4.4 multiply_reduce_fusion.2
  645.0 2.0 fusion.46
  647.1 2.9 fusion.47
  651.0 10.4 %gather_fusion = bf16[192,128,128]{2,1,0:T(8,128)(2,1)} fusion(bf16[144,128,128]{2,1,0:T(8,128)(2,1)} %get-tuple-element.132, s32[1024]{0:T(1024)S(1)} %pad_clamp_fusion.3), kind=kCustom, calls=%fused_computation.clone.1 | custom fusion | bytes 12583680 | tf_op jit(solution)/shard_map/while/body/eval_jaxpr/gather | solution.py:76
  661.4 8.6 %copy.187 = bf16[192,128,128]{1,2,0:T(8,128)(2,1)} copy(bf16[192,128,128]{2,1,0:T(8,128)(2,1)} %gather_fusion) | data formatting | bytes 12582912 | tf_op jit(solution)/shard_map/while/body/eval_jaxpr/gather | solution.py:76
  671.2 4.4 multiply_reduce_fusion.2
  677.6 2.9 fusion.47
  681.5 10.4 %gather_fusion = bf16[192,128,128]{2,1,0:T(8,128)(2,1)} fusion(bf16[144,128,128]{2,1,0:T(8,128)(2,1)} %get-tuple-element.132, s32[1024]{0:T(1024)S(1)} %pad_clamp_fusion.3), kind=kCustom, calls=%fused_computation.clone.1 | custom fusion | bytes 12583680 | tf_op jit(solution)/shard_map/while/body/eval_jaxpr/gather | solution.py:76
  691.9 8.6 %copy.187 = bf16[192,128,128]{1,2,0:T(8,128)(2,1)} copy(bf16[192,128,128]{2,1,0:T(8,128)(2,1)} %gather_fusion) | data formatting | bytes 12582912 | tf_op jit(solution)/shard_map/while/body/eval_jaxpr/gather | solution.py:76
  701.7 4.4 multiply_reduce_fusion.2
  706.0 2.0 fusion.46
  708.1 2.9 fusion.47
  712.0 10.4 %gather_fusion = bf16[192,128,128]{2,1,0:T(8,128)(2,1)} fusion(bf16[144,128,128]{2,1,0:T(8,128)(2,1)} %get-tuple-element.132, s32[1024]{0:T(1024)S(1)} %pad_clamp_fusion.3), kind=kCustom, calls=%fused_computation.clone.1 | custom fusion | bytes 12583680 | tf_op jit(solution)/shard_map/while/body/eval_jaxpr/gather | solution.py:76
  722.4 8.6 %copy.187 = bf16[192,128,128]{1,2,0:T(8,128)(2,1)} copy(bf16[192,128,128]{2,1,0:T(8,128)(2,1)} %gather_fusion) | data formatting | bytes 12582912 | tf_op jit(solution)/shard_map/while/body/eval_jaxpr/gather | solution.py:76
  732.1 4.4 multiply_reduce_fusion.2
  736.5 2.0 fusion.46
  738.6 2.9 fusion.47
  742.4 2.8 all_to_all.65
  746.4 32.2 %all_to_all.73 = bf16[16,1024,64]{1,2,0:T(8,128)(2,1)S(1)} all-to-all(bf16[16,1024,64]{1,2,0:T(8,128)(2,1)S(1)} %copy.158), channel_id=1, replica_groups=mesh['ctx'=8,'head'=16] {'head'}, dimensions={0} | all-to-all | bytes 4194304 | tf_op jit(solution)/shard_map/all_to_all | solution.py:95
  778.5 2.5 copy.159
  (125 shorter events, 31.4 us)
Async XLA Ops:
  11.3 35.0 %all-to-all-start.1 = ((bf16[1024,16,64]{0,2,1:T(8,128)(2,1)}), bf16[1024,16,64]{0,2,1:T(8,128)(2,1)S(1)}, u32[]{:S(2)}, u32[]{:S(2)}) async-start(bf16[1024,16,64]{0,2,1:T(8,128)(2,1)} %bitcast.99), calls=%async_computation.1 | async-start | bytes 4194304 | tf_op jit(solution)/shard_map/all_to_all | solution.py:17
  19.1 32.2 %copy-start.2 = (s32[1,128,12]{1,0,2:T(1,128)S(1)}, s32[1,128,12]{1,0,2:T(1,128)}, u32[]{:S(2)}) copy-start(s32[1,128,12]{1,0,2:T(1,128)} %param.9) | copy-start | bytes 18436
  46.3 32.3 %all-to-all-start.2 = ((bf16[1024,16,64]{0,2,1:T(8,128)(2,1)}), bf16[1024,16,64]{0,2,1:T(8,128)(2,1)}, u32[]{:S(2)}, u32[]{:S(2)}) async-start(bf16[1024,16,64]{0,2,1:T(8,128)(2,1)} %bitcast.98), calls=%async_computation.2 | async-start | bytes 4194304 | tf_op jit(solution)/shard_map/all_to_all | solution.py:18
  51.3 41.6 %top_k.22.cloned.1.call-start = ((), (), s32[]{:S(2)}) async-start(), calls=%async_computation.5 | async-start | bytes 24608 | tf_op jit(solution)/shard_map/top_k | solution.py:37
  53.8 386.5 %all-gather.2.cloned.1.call-start = ((), (), s32[]{:S(2)}) async-start(), calls=%async_computation.4 | async-start | bytes 37748736 | tf_op jit(solution)/shard_map/all_gather | solution.py:46
  78.6 2.2 copy-start.1
  87.3 48.7 %all-to-all-start = ((bf16[1024,16,64]{0,2,1:T(8,128)(2,1)}), bf16[1024,16,64]{0,2,1:T(8,128)(2,1)}, u32[]{:S(2)}, u32[]{:S(2)}) async-start(bf16[1024,16,64]{0,2,1:T(8,128)(2,1)} %bitcast.97), calls=%async_computation | async-start | bytes 4194304 | tf_op jit(solution)/shard_map/all_to_all | solution.py:16
  141.0 345.4 %copy-start = (bf16[128,128,64]{1,0,2:T(8,128)(2,1)S(1)}, bf16[128,128,64]{1,0,2:T(8,128)(2,1)}, u32[]{:S(2)}) copy-start(bf16[128,128,64]{1,0,2:T(8,128)(2,1)} %concatenate.16) | copy-start | bytes 6291460
  517.6 7.6 slice-start
  518.7 6.4 slice-start.1
  548.1 7.6 slice-start
  549.2 6.4 slice-start.1
  578.5 7.5 slice-start
  579.7 6.4 slice-start.1
  609.0 7.6 slice-start
  610.2 6.4 slice-start.1
  639.5 7.6 slice-start
  640.7 6.4 slice-start.1
  670.0 7.6 slice-start
  671.1 6.4 slice-start.1
  700.5 7.6 slice-start
  701.6 6.4 slice-start.1
  731.0 7.6 slice-start
  732.1 6.4 slice-start.1
Sparse Core Ops, SparseCore 0:
  54.4 2.2 top_k.24.cloned.1.call-done
  (1 shorter events, 0.0 us)
Sparse Core Ops, SparseCore 1:
  83.4 356.8 all-gather.1
where the time goes:
time: 792 us; the launch traced here: 789 us
  waiting for transfers between devices  372 us (47%)
  local copies, waits for them, and re-layouts  265 us (33%)
  matrix products  58 us (7%)
  blocking collectives  32.2 us (4%)
  other arithmetic  27.4 us (3%)
  starting transfers between devices  18 us (2%)
  between operations  15 us (2%)
    all_gather x1, waiting for transfers between devices, on_device(): piece = lax.all_gather(kv_pack, 'ctx', axis=0, tiled=True)  299 us
    gather x16, local copies, waits for them, and re-layouts, attend(): picked = kv_table[idx_grp]  152 us
    all_gather x1, local copies, waits for them, and re-layouts, on_device(): piece = lax.all_gather(kv_pack, 'ctx', axis=0, tiled=True)  44 us
    dot_general x8, matrix products, attend(): jnp.einsum('gqd,gjkd->gqjk', q_grp, picked[..., :DH], preferred_element_t...  34.8 us
    all_to_all x1, blocking collectives, on_device(): lax.all_to_all(head_outputs, 'head', split_axis=0, concat_axis=1, tiled=T...  32.2 us
    all_to_all x1, waiting for transfers between devices, on_device(): lax.all_to_all(query, 'head', split_axis=1, concat_axis=0, tiled=True)  26.3 us
    all_to_all x1, waiting for transfers between devices, on_device(): lax.all_to_all(value, 'head', split_axis=1, concat_axis=0, tiled=True)  23.2 us
    dot_general x8, matrix products, attend(): jnp.einsum('gqjk,gjkd->gqd', exp_scores.astype(jnp.bfloat16), picked[...,...  23.2 us
  transfers between devices with their start and end apart: 4, of which 4 were waited for; matrix products, arithmetic and copies ran while one was open for 4% of the time, Pallas kernels for 0%

commit v1 on v0

v1 whole, which is shorter than its diff:
```python
import functools

import jax
import jax.numpy as jnp
from jax import lax
from jax.experimental import pallas as pl
from jax.experimental.pallas import tpu as pltpu
from jax.sharding import PartitionSpec as P

DH = 64
BLK = 128
KPER = 12
PMOST = 2
LANES = 2 * DH
NT = (((1,), (1,)), ((), ()))
NN = (((1,), (0,)), ((), ()))
VMEM_LIMIT = 48 * 1024 * 1024


def pack_kv(key, value):
    tok, width = key.shape

    def body(k_ref, v_ref, o_ref):
        k, v = k_ref[...], v_ref[...]
        o_ref[0] = jnp.concatenate([k[:, :DH], v[:, :DH]], axis=1)
        o_ref[1] = jnp.concatenate([k[:, DH:], v[:, DH:]], axis=1)

    spec = pl.BlockSpec((tok, LANES), lambda c: (0, c))
    return pl.pallas_call(
        body,
        grid=(width // LANES,),
        in_specs=[spec, spec],
        out_specs=pl.BlockSpec((2, tok, LANES), lambda c: (c, 0, 0)),
        out_shape=jax.ShapeDtypeStruct((width // DH, tok, LANES), jnp.bfloat16),
        cost_estimate=pl.CostEstimate(flops=0, bytes_accessed=8 * tok * width, transcendentals=0),
        name="pack_kv",
    )(key, value)


def pack_q(query, chunks):
    tok, width = query.shape
    pairs = tok // (2 * BLK)
    per = pairs // chunks

    def body(q_ref, *outs):
        for p in range(pairs):
            o_ref = outs[p // per]
            a = q_ref[2 * p * BLK : (2 * p + 1) * BLK, :] * jnp.bfloat16(0.125)
            b = q_ref[(2 * p + 1) * BLK : (2 * p + 2) * BLK, :] * jnp.bfloat16(0.125)
            o_ref[0, p % per] = jnp.concatenate([a[:, :DH], b[:, :DH]], axis=1)
            o_ref[1, p % per] = jnp.concatenate([a[:, DH:], b[:, DH:]], axis=1)

    shape = jax.ShapeDtypeStruct((width // DH, per, BLK, LANES), jnp.bfloat16)
    return pl.pallas_call(
        body,
        grid=(width // LANES,),
        in_specs=[pl.BlockSpec((tok, LANES), lambda c: (0, c))],
        out_specs=[pl.BlockSpec((2, per, BLK, LANES), lambda c: (c, 0, 0, 0))] * chunks,
        out_shape=[shape] * chunks,
        cost_estimate=pl.CostEstimate(flops=0, bytes_accessed=4 * tok * width, transcendentals=0),
        name="pack_q",
    )(query)


def pick_blocks(kv_blocks, wanted):
    count = wanted.shape[0]

    def body(w_ref, kv_ref, o_ref, sem):
        copies = [
            pltpu.make_async_copy(kv_ref.at[w_ref[i]], o_ref.at[i], sem.at[i]) for i in range(count)
        ]
        for c in copies:
            c.start()
        for c in copies:
            c.wait()

    return pl.pallas_call(
        body,
        in_specs=[
            pl.BlockSpec(memory_space=pltpu.SMEM),
            pl.BlockSpec(memory_space=pl.ANY),
        ],
        out_specs=pl.BlockSpec(memory_space=pl.ANY),
        out_shape=jax.ShapeDtypeStruct((count,) + kv_blocks.shape[1:], jnp.bfloat16),
        scratch_shapes=[pltpu.SemaphoreType.DMA((count,))],
        cost_estimate=pl.CostEstimate(
            flops=0, bytes_accessed=count * BLK * LANES * 4, transcendentals=0
        ),
        name="pick_blocks",
    )(wanted, kv_blocks)


def attend(table_index, q_pairs, kv_local, kv_remote, first_block, per_source):
    sources, per = q_pairs.shape[:2]
    pairs = sources * per
    nlocal, nremote = kv_local.shape[0], kv_remote.shape[0]
    q_flat = q_pairs.reshape(pairs, BLK, LANES)

    def body(idx_ref, q_ref, loc_ref, rem_ref, o_ref, tab, s_buf, m_buf, sems):
        c0 = pltpu.make_async_copy(loc_ref, tab.at[pl.ds(0, nlocal)], sems.at[0])
        c1 = pltpu.make_async_copy(rem_ref, tab.at[pl.ds(nlocal, nremote)], sems.at[1])
        c0.start()
        c1.start()
        c0.wait()
        c1.wait()
        zeros = jnp.zeros((BLK, DH), jnp.bfloat16)

        def entry(pair, half):
            block = (pair // per) * per_source + first_block + 2 * (pair % per) + half
            return block * KPER

        def keys_of(base, jj):
            return jnp.concatenate(
                [tab[idx_ref[base + 2 * jj]], tab[idx_ref[base + 2 * jj + 1]]], axis=0
            )

        def score(pair, half):
            base = entry(pair, half)
            q = jnp.concatenate([q_ref[pair, :, half * DH : (half + 1) * DH], zeros], axis=1)
            top = None
            for jj in range(KPER // 2):
                s = lax.dot_general(q, keys_of(base, jj), NT, preferred_element_type=jnp.float32)
                s_buf[half, :, jj * 2 * BLK : (jj + 1) * 2 * BLK] = s
                both = jnp.maximum(s[:, :BLK], s[:, BLK:])
                top = both if top is None else jnp.maximum(top, both)
            m_buf[half] = jnp.broadcast_to(jnp.max(top, axis=1, keepdims=True), (BLK, LANES))

        def finish(pair, half):
            base = entry(pair, half)
            top = m_buf[half]
            top2 = jnp.concatenate([top, top], axis=1)
            total, acc = None, None
            for jj in range(KPER // 2):
                p = jnp.exp(s_buf[half, :, jj * 2 * BLK : (jj + 1) * 2 * BLK] - top2)
                both = p[:, :BLK] + p[:, BLK:]
                total = both if total is None else total + both
                part = lax.dot_general(
                    p.astype(jnp.bfloat16),
                    keys_of(base, jj),
                    NN,
                    preferred_element_type=jnp.float32,
                )
                acc = part if acc is None else acc + part
            total = jnp.sum(total, axis=1, keepdims=True)
            return (acc[:, DH:] / total).astype(jnp.bfloat16)

        score(0, 0)

        def step(i, carry):
            score(i, 1)
            a = finish(i, 0)
            score(jnp.minimum(i + 1, pairs - 1), 0)
            b = finish(i, 1)
            o_ref[i] = jnp.concatenate([a, b], axis=1)
            return carry

        lax.fori_loop(0, pairs, step, 0)

    out = pl.pallas_call(
        body,
        in_specs=[
            pl.BlockSpec(memory_space=pltpu.SMEM),
            pl.BlockSpec(memory_space=pltpu.VMEM),
            pl.BlockSpec(memory_space=pl.ANY),
            pl.BlockSpec(memory_space=pl.ANY),
        ],
        out_specs=pl.BlockSpec(memory_space=pltpu.VMEM),
        out_shape=jax.ShapeDtypeStruct((pairs, BLK, LANES), jnp.bfloat16),
        scratch_shapes=[
            pltpu.VMEM((nlocal + nremote, BLK, LANES), jnp.bfloat16),
            pltpu.VMEM((2, BLK, KPER * BLK), jnp.float32),
            pltpu.VMEM((2, BLK, LANES), jnp.float32),
            pltpu.SemaphoreType.DMA((2,)),
        ],
        compiler_params=pltpu.CompilerParams(vmem_limit_bytes=VMEM_LIMIT),
        cost_estimate=pl.CostEstimate(
            flops=pairs * 2 * KPER * BLK * BLK * LANES * 4,
            bytes_accessed=(nlocal + nremote + 2 * pairs) * BLK * LANES * 2,
            transcendentals=pairs * 2 * KPER * BLK * BLK,
        ),
        name="attend",
    )(table_index, q_flat, kv_local, kv_remote)
    return out.reshape(sources, per, BLK, LANES)


def unpack(o_pairs, tok, width, first_pair, into):
    heads, per = o_pairs.shape[:2]
    rows = per * 2 * BLK

    def body(o_ref, *rest):
        out_ref = rest[-1]
        for p in range(per):
            even, odd = o_ref[0, p], o_ref[1, p]
            out_ref[2 * p * BLK : (2 * p + 1) * BLK, :] = jnp.concatenate(
                [even[:, :DH], odd[:, :DH]], axis=1
            )
            out_ref[(2 * p + 1) * BLK : (2 * p + 2) * BLK, :] = jnp.concatenate(
                [even[:, DH:], odd[:, DH:]], axis=1
            )

    row_block = first_pair // per
    in_specs = [pl.BlockSpec((2, per, BLK, LANES), lambda c: (c, 0, 0, 0))]
    args = [o_pairs]
    if into is not None:
        in_specs.append(pl.BlockSpec(memory_space=pl.ANY))
        args.append(into)
    return pl.pallas_call(
        body,
        grid=(width // LANES,),
        in_specs=in_specs,
        out_specs=pl.BlockSpec((rows, LANES), lambda c: (row_block, c)),
        out_shape=jax.ShapeDtypeStruct((tok, width), jnp.bfloat16),
        input_output_aliases={1: 0} if into is not None else {},
        cost_estimate=pl.CostEstimate(flops=0, bytes_accessed=4 * rows * width, transcendentals=0),
        name="unpack",
    )(*args)


def across(x, axis):
    return lax.all_to_all(x, axis, split_axis=0, concat_axis=0, tiled=True)


def on_device(chunks, query, key, value, pattern):
    tok, width = query.shape
    sources = lax.axis_size("head")
    ranges = lax.axis_size("ctx")
    own = lax.axis_index("ctx")
    per_source = tok // BLK
    count = sources * per_source

    kv_send = pack_kv(key, value)
    kv_blocks = across(kv_send, "head").reshape(count, BLK, LANES)
    q_send = pack_q(query, chunks)

    rows = pattern[0]
    owner, pos = rows // count, rows % count
    of_range = owner[None] == jnp.arange(ranges, dtype=jnp.int32)[:, None, None]
    low = jnp.min(jnp.where(of_range, pos[None], count - 1), axis=(1, 2))
    high = jnp.max(jnp.where(of_range, pos[None], 0), axis=(1, 2))
    wanted = jnp.stack([low, high], axis=1)
    slot = jnp.sum(jnp.where(of_range, (pos[None] != low[:, None, None]).astype(jnp.int32), 0), axis=0)
    table_index = jnp.where(owner == own, pos, count + owner * PMOST + slot).reshape(-1)
    asked = lax.all_gather(wanted, "ctx", axis=0)
    asked = lax.dynamic_index_in_dim(asked, own, axis=1, keepdims=False).reshape(-1)

    picked = pick_blocks(kv_blocks, asked)
    remote = across(picked.reshape(ranges, PMOST * BLK, LANES), "ctx")
    remote = remote.reshape(ranges * PMOST, BLK, LANES)

    out = None
    per = per_source // (2 * chunks)
    for c in range(chunks):
        q_pairs = across(q_send[c], "head")
        o_pairs = attend(table_index, q_pairs, kv_blocks, remote, 2 * per * c, per_source)
        o_pairs = across(o_pairs, "head")
        out = unpack(o_pairs, tok, width, per * c, out)
    return out


def solution(mesh):
    placed = (
        P(("ctx", "head"), None),
        P(("ctx", "head"), None),
        P(("ctx", "head"), None),
        P("head", "ctx", None),
    )
    return jax.shard_map(
        functools.partial(on_device, 2),
        mesh=mesh,
        in_specs=placed,
        out_specs=P(("ctx", "head"), None),
        check_vma=False,
    )
```

time: 792 us -> 225 us (0.28)
  waiting for transfers between devices: 372 us -> 54 us
  local copies, waits for them, and re-layouts: 265 us -> 2.31 us
  Pallas kernels: 0 us -> 96.4 us
  matrix products: 58 us -> 0 us
  other arithmetic: 27.4 us -> 0.36 us
  starting transfers between devices: 18 us -> 33.2 us
  between operations: 15 us -> 0.14 us
    all_gather x1 -> x0, waiting for transfers between devices: 299 us -> none  [on_device(): piece = lax.all_gather(kv_pack, 'ctx', axis=0, tiled=True)]
    gather x20 -> x0, local copies, waits for them, and re-layouts: 157 us -> none  [the longest x16 152 us: attend(): picked = kv_table[idx_grp]]
    pallas_call x0 -> x7, Pallas kernels: none -> 96.4 us  [the longest x2 54.4 us: attend(): pl.pallas_call(body, in_specs=[pl.BlockSpec(memory_space=pltpu.SMEM), pl....]
    dot_general x16 -> x0, matrix products: 58 us -> none  [the longest x8 34.8 us: attend(): jnp.einsum('gqd,gjkd->gqjk', q_grp, picked[..., :DH], preferred_element_t...]
    all_gather x1 -> x0, local copies, waits for them, and re-layouts: 44 us -> none  [on_device(): piece = lax.all_gather(kv_pack, 'ctx', axis=0, tiled=True)]
    all_gather x0 -> x1, blocking collectives: none -> 25.2 us  [on_device(): asked = lax.all_gather(wanted, 'ctx', axis=0)]
    all_to_all x1, blocking collectives: 32.2 us -> 12.2 us  [across(): return lax.all_to_all(x, axis, split_axis=0, concat_axis=0, tiled=True)]
    all_to_all x3 -> x5, waiting for transfers between devices: 72.7 us -> 54 us  [across(): return lax.all_to_all(x, axis, split_axis=0, concat_axis=0, tiled=True)]
  transfers between devices with their start and end apart: 4 -> 5, of which waited for: 4 -> 2; matrix products, arithmetic and copies ran while one was open for 4% -> 1% of each run, Pallas kernels for 0% -> 37%
where the time goes in v1:
time: 225 us; the launch traced here: 224 us
  Pallas kernels  96.4 us (43%)
  waiting for transfers between devices  54 us (24%)
  blocking collectives  37.4 us (17%)
  starting transfers between devices  33.2 us (15%)
  local copies, waits for them, and re-layouts  2.31 us (1%)
    pallas_call x2, Pallas kernels, attend(): pl.pallas_call(body, in_specs=[pl.BlockSpec(memory_space=pltpu.SMEM), pl....  54.4 us
    all_to_all x5, waiting for transfers between devices, across(): return lax.all_to_all(x, axis, split_axis=0, concat_axis=0, tiled=True)  54 us
    all_to_all x5, starting transfers between devices, across(): return lax.all_to_all(x, axis, split_axis=0, concat_axis=0, tiled=True)  33.2 us
    all_gather x1, blocking collectives, on_device(): asked = lax.all_gather(wanted, 'ctx', axis=0)  25.2 us
    pallas_call x1, Pallas kernels, pick_blocks(): pl.pallas_call(body, in_specs=[pl.BlockSpec(memory_space=pltpu.SMEM), pl....  17.8 us
    all_to_all x1, blocking collectives, across(): return lax.all_to_all(x, axis, split_axis=0, concat_axis=0, tiled=True)  12.2 us
    pallas_call x2, Pallas kernels, unpack(): pl.pallas_call(body, grid=(width // LANES,), in_specs=in_specs, out_specs...  11 us
    pallas_call x1, Pallas kernels, pack_kv(): pl.pallas_call(body, grid=(width // LANES,), in_specs=[spec, spec], out_s...  7.27 us
  transfers between devices with their start and end apart: 5, of which 2 were waited for; matrix products, arithmetic and copies ran while one was open for 1% of the time, Pallas kernels for 37%

profile of v1, /device:TPU:1, one launch (start us, length us, event | category | flops | bytes accessed | tf_op | source)
XLA Modules:
  0.0 223.9 jit_solution(15621037000087587416)
XLA Ops:
  0.0 7.3 %pack_kv.1 = bf16[16,1024,128]{2,1,0:T(8,128)(2,1)} custom-call(bf16[1024,1024]{1,0:T(8,128)(2,1)} %k_ref.1, bf16[1024,1024]{1,0:T(8,128)(2,1)} %v_ref.1), custom_call_target="tpu_custom_call" | custom-call | bytes 8388608 | tf_op jit(solution)/shard_map/pack_kv/pallas_call | solution.py:29
  7.3 7.8 %all-to-all-start.1 = ((bf16[16,1024,128]{2,1,0:T(8,128)(2,1)}), bf16[16,1024,128]{2,1,0:T(8,128)(2,1)}, u32[]{:S(2)}, u32[]{:S(2)}) async-start(bf16[16,1024,128]{2,1,0:T(8,128)(2,1)} %pack_kv.1), calls=%async_computation.1 | async-start | bytes 8388608 | tf_op jit(solution)/shard_map/all_to_all | solution.py:220
  15.1 0.0 copy-start.2
  15.1 5.9 %pack_q.1 = (bf16[16,2,128,128]{3,2,1,0:T(8,128)(2,1)}, bf16[16,2,128,128]{3,2,1,0:T(8,128)(2,1)}) custom-call(bf16[1024,1024]{1,0:T(8,128)(2,1)} %q_ref.1), custom_call_target="tpu_custom_call" | custom-call | bytes 4194304 | tf_op jit(solution)/shard_map/pack_q/pallas_call | solution.py:54
  21.1 43.7 %all-to-all-done.1 = bf16[16,1024,128]{2,1,0:T(8,128)(2,1)} async-done(((bf16[16,1024,128]{2,1,0:T(8,128)(2,1)}), bf16[16,1024,128]{2,1,0:T(8,128)(2,1)}, u32[]{:S(2)}, u32[]{:S(2)}) %all-to-all-start.1) | async-done | bytes 4194336 | tf_op jit(solution)/shard_map/all_to_all | solution.py:220
  64.8 4.3 %all-to-all-start.4 = ((bf16[16,2,128,128]{3,2,1,0:T(8,128)(2,1)}), bf16[16,2,128,128]{3,2,1,0:T(8,128)(2,1)S(1)}, u32[]{:S(2)}, u32[]{:S(2)}) async-start(bf16[16,2,128,128]{3,2,1,0:T(8,128)(2,1)} %get-tuple-element.8), calls=%async_computation.4 | async-start | bytes 2097152 | tf_op jit(solution)/shard_map/all_to_all | solution.py:220
  69.1 0.0 copy-done.2
  69.2 0.1 select_reduce_fusion.2
  69.3 0.2 select_reduce_fusion
  69.5 25.2 %all-gather.1 = s32[8,8,2]{1,2,0:T(2,128)S(1)} all-gather(s32[1,8,2]{1,2,0:T(2,128)S(1)} %add_bitcast_fusion), channel_id=2, replica_groups=mesh['ctx'=8,'head'=16] {'ctx'}, dimensions={0}, use_global_device_ids=true | all-gather | bytes 576 | tf_op jit(solution)/shard_map/all_gather | solution.py:243
  94.7 0.3 dynamic-slice_reduce_fusion
  95.0 0.6 reshape.31.w_ref
  95.6 17.8 %pick_blocks.1 = bf16[16,128,128]{2,1,0:T(8,128)(2,1)} custom-call(s32[16]{0:T(128)} %reshape.31.w_ref, bf16[128,128,128]{2,1,0:T(8,128)(2,1)} %bitcast.1.kv_ref.loc_ref), custom_call_target="tpu_custom_call" | custom-call | bytes 1048576 | tf_op jit(solution)/shard_map/pick_blocks/pallas_call | solution.py:77
  113.4 0.0 all-to-all-done.4
  113.4 12.2 %all_to_all.30 = bf16[8,256,128]{2,1,0:T(8,128)(2,1)S(1)} all-to-all(bf16[8,256,128]{2,1,0:T(8,128)(2,1)} %bitcast.19), channel_id=1, replica_groups=mesh['ctx'=8,'head'=16] {'ctx'}, dimensions={0} | all-to-all | bytes 1048576 | tf_op jit(solution)/shard_map/all_to_all | solution.py:220
  125.6 9.8 %all-to-all-start = ((bf16[16,2,128,128]{3,2,1,0:T(8,128)(2,1)}), bf16[16,2,128,128]{3,2,1,0:T(8,128)(2,1)S(1)}, u32[]{:S(2)}, u32[]{:S(2)}) async-start(bf16[16,2,128,128]{3,2,1,0:T(8,128)(2,1)} %get-tuple-element.7), calls=%async_computation | async-start | bytes 2097152 | tf_op jit(solution)/shard_map/all_to_all | solution.py:220
  135.4 0.1 copy.14
  135.5 0.1 copy.15
  135.6 0.1 reduce_sum.12
  135.7 0.1 squeeze.5
  135.8 27.2 %attend.3 = bf16[32,128,128]{2,1,0:T(8,128)(2,1)} custom-call(s32[1536]{0:T(1024)S(1)} %fusion.idx_ref, bf16[32,128,128]{2,1,0:T(8,128)(2,1)S(1)} %bitcast.15, bf16[128,128,128]{2,1,0:T(8,128)(2,1)} %bitcast.1.kv_ref.loc_ref, bf16[16,128,128]{2,1,0:T(8,128)(2,1)S(1)} %bitcast.17), custom_call_target="tpu_custom_call" | custom-call | flops 6442450944 | bytes 6815744 | tf_op jit(solution)/shard_map/attend/pallas_call | solution.py:159
  163.0 0.0 all-to-all-done
  163.0 5.7 %all-to-all-start.5 = ((bf16[16,2,128,128]{3,2,1,0:T(8,128)(2,1)}), bf16[16,2,128,128]{3,2,1,0:T(8,128)(2,1)S(1)}, u32[]{:S(2)}, u32[]{:S(2)}) async-start(bf16[16,2,128,128]{3,2,1,0:T(8,128)(2,1)} %bitcast.9), calls=%async_computation.5 | async-start | bytes 2097152 | tf_op jit(solution)/shard_map/all_to_all | solution.py:220
  168.7 27.2 %attend.2 = bf16[32,128,128]{2,1,0:T(8,128)(2,1)} custom-call(s32[1536]{0:T(1024)S(1)} %fusion.idx_ref, bf16[32,128,128]{2,1,0:T(8,128)(2,1)S(1)} %bitcast.16, bf16[128,128,128]{2,1,0:T(8,128)(2,1)} %bitcast.1.kv_ref.loc_ref, bf16[16,128,128]{2,1,0:T(8,128)(2,1)S(1)} %bitcast.18), custom_call_target="tpu_custom_call" | custom-call | flops 6442450944 | bytes 6815744 | tf_op jit(solution)/shard_map/attend/pallas_call | solution.py:159
  195.9 0.0 all-to-all-done.5.o_ref
  196.0 0.0 copy-start
  196.0 5.6 %all-to-all-start.3 = ((bf16[16,2,128,128]{3,2,1,0:T(8,128)(2,1)}), bf16[16,2,128,128]{3,2,1,0:T(8,128)(2,1)S(1)}, u32[]{:S(2)}, u32[]{:S(2)}) async-start(bf16[16,2,128,128]{3,2,1,0:T(8,128)(2,1)} %bitcast.7), calls=%async_computation.3 | async-start | bytes 2097152 | tf_op jit(solution)/shard_map/all_to_all | solution.py:220
  201.6 0.0 copy-done
  201.6 5.5 %unpack.2.rest_0_ = bf16[1024,1024]{1,0:T(8,128)(2,1)} custom-call(bf16[16,2,128,128]{3,2,1,0:T(8,128)(2,1)} %copy-done), custom_call_target="tpu_custom_call" | custom-call | bytes 2097152 | tf_op jit(solution)/shard_map/unpack/pallas_call | solution.py:207
  207.1 10.3 %all-to-all-done.3.o_ref = bf16[16,2,128,128]{3,2,1,0:T(8,128)(2,1)S(1)} async-done(((bf16[16,2,128,128]{3,2,1,0:T(8,128)(2,1)}), bf16[16,2,128,128]{3,2,1,0:T(8,128)(2,1)S(1)}, u32[]{:S(2)}, u32[]{:S(2)}) %all-to-all-start.3) | async-done | bytes 1048608 | tf_op jit(solution)/shard_map/all_to_all | solution.py:220
  217.4 0.0 copy-start.1
  217.4 1.0 copy-done.1
  218.4 5.5 %unpack.3 = bf16[1024,1024]{1,0:T(8,128)(2,1)} custom-call(bf16[16,2,128,128]{3,2,1,0:T(8,128)(2,1)} %copy-done.1, bf16[1024,1024]{1,0:T(8,128)(2,1)} %unpack.2.rest_0_), custom_call_target="tpu_custom_call", output_to_operand_aliasing={{}: (1, {})} | custom-call | bytes 2097152 | tf_op jit(solution)/shard_map/unpack/pallas_call | solution.py:207
  (5 shorter events, 0.1 us)
Async XLA Ops:
  7.3 57.5 %all-to-all-start.1 = ((bf16[16,1024,128]{2,1,0:T(8,128)(2,1)}), bf16[16,1024,128]{2,1,0:T(8,128)(2,1)}, u32[]{:S(2)}, u32[]{:S(2)}) async-start(bf16[16,1024,128]{2,1,0:T(8,128)(2,1)} %pack_kv.1), calls=%async_computation.1 | async-start | bytes 8388608 | tf_op jit(solution)/shard_map/all_to_all | solution.py:220
  15.1 54.0 %copy-start.2 = (s32[1,128,12]{1,0,2:T(1,128)S(1)}, s32[1,128,12]{1,0,2:T(1,128)}, u32[]{:S(2)}) copy-start(s32[1,128,12]{1,0,2:T(1,128)} %param.7) | copy-start | bytes 18436
  64.8 48.6 %all-to-all-start.4 = ((bf16[16,2,128,128]{3,2,1,0:T(8,128)(2,1)}), bf16[16,2,128,128]{3,2,1,0:T(8,128)(2,1)S(1)}, u32[]{:S(2)}, u32[]{:S(2)}) async-start(bf16[16,2,128,128]{3,2,1,0:T(8,128)(2,1)} %get-tuple-element.8), calls=%async_computation.4 | async-start | bytes 2097152 | tf_op jit(solution)/shard_map/all_to_all | solution.py:220
  125.6 37.4 %all-to-all-start = ((bf16[16,2,128,128]{3,2,1,0:T(8,128)(2,1)}), bf16[16,2,128,128]{3,2,1,0:T(8,128)(2,1)S(1)}, u32[]{:S(2)}, u32[]{:S(2)}) async-start(bf16[16,2,128,128]{3,2,1,0:T(8,128)(2,1)} %get-tuple-element.7), calls=%async_computation | async-start | bytes 2097152 | tf_op jit(solution)/shard_map/all_to_all | solution.py:220
  163.0 32.9 %all-to-all-start.5 = ((bf16[16,2,128,128]{3,2,1,0:T(8,128)(2,1)}), bf16[16,2,128,128]{3,2,1,0:T(8,128)(2,1)S(1)}, u32[]{:S(2)}, u32[]{:S(2)}) async-start(bf16[16,2,128,128]{3,2,1,0:T(8,128)(2,1)} %bitcast.9), calls=%async_computation.5 | async-start | bytes 2097152 | tf_op jit(solution)/shard_map/all_to_all | solution.py:220
  196.0 5.6 %copy-start = (bf16[16,2,128,128]{3,2,1,0:T(8,128)(2,1)}, bf16[16,2,128,128]{3,2,1,0:T(8,128)(2,1)S(1)}, u32[]{:S(2)}) copy-start(bf16[16,2,128,128]{3,2,1,0:T(8,128)(2,1)S(1)} %all-to-all-done.5.o_ref) | copy-start | bytes 3145732
  196.0 21.4 %all-to-all-start.3 = ((bf16[16,2,128,128]{3,2,1,0:T(8,128)(2,1)}), bf16[16,2,128,128]{3,2,1,0:T(8,128)(2,1)S(1)}, u32[]{:S(2)}, u32[]{:S(2)}) async-start(bf16[16,2,128,128]{3,2,1,0:T(8,128)(2,1)} %bitcast.7), calls=%async_computation.3 | async-start | bytes 2097152 | tf_op jit(solution)/shard_map/all_to_all | solution.py:220
  217.4 1.0 copy-start.1

commit v2 on v1

--- a/solution.py
+++ b/solution.py
@@ -19,45 +19,49 @@
 
 def pack_kv(key, value):
     tok, width = key.shape
+    rows = tok // 2
 
     def body(k_ref, v_ref, o_ref):
-        k, v = k_ref[...], v_ref[...]
-        o_ref[0] = jnp.concatenate([k[:, :DH], v[:, :DH]], axis=1)
-        o_ref[1] = jnp.concatenate([k[:, DH:], v[:, DH:]], axis=1)
-
-    spec = pl.BlockSpec((tok, LANES), lambda c: (0, c))
-    return pl.pallas_call(
-        body,
-        grid=(width // LANES,),
+        for c in range(width // LANES):
+            k = k_ref[:, c * LANES : (c + 1) * LANES]
+            v = v_ref[:, c * LANES : (c + 1) * LANES]
+            o_ref[2 * c] = jnp.concatenate([k[:, :DH], v[:, :DH]], axis=1)
+            o_ref[2 * c + 1] = jnp.concatenate([k[:, DH:], v[:, DH:]], axis=1)
+
+    spec = pl.BlockSpec((rows, width), lambda i: (i, 0))
+    return pl.pallas_call(
+        body,
+        grid=(tok // rows,),
         in_specs=[spec, spec],
-        out_specs=pl.BlockSpec((2, tok, LANES), lambda c: (c, 0, 0)),
+        out_specs=pl.BlockSpec((width // DH, rows, LANES), lambda i: (0, i, 0)),
         out_shape=jax.ShapeDtypeStruct((width // DH, tok, LANES), jnp.bfloat16),
+        compiler_params=pltpu.CompilerParams(vmem_limit_bytes=VMEM_LIMIT),
         cost_estimate=pl.CostEstimate(flops=0, bytes_accessed=8 * tok * width, transcendentals=0),
         name="pack_kv",
     )(key, value)
 
 
-def pack_q(query, chunks):
-    tok, width = query.shape
-    pairs = tok // (2 * BLK)
-    per = pairs // chunks
-
-    def body(q_ref, *outs):
-        for p in range(pairs):
-            o_ref = outs[p // per]
-            a = q_ref[2 * p * BLK : (2 * p + 1) * BLK, :] * jnp.bfloat16(0.125)
-            b = q_ref[(2 * p + 1) * BLK : (2 * p + 2) * BLK, :] * jnp.bfloat16(0.125)
-            o_ref[0, p % per] = jnp.concatenate([a[:, :DH], b[:, :DH]], axis=1)
-            o_ref[1, p % per] = jnp.concatenate([a[:, DH:], b[:, DH:]], axis=1)
-
-    shape = jax.ShapeDtypeStruct((width // DH, per, BLK, LANES), jnp.bfloat16)
-    return pl.pallas_call(
-        body,
-        grid=(width // LANES,),
-        in_specs=[pl.BlockSpec((tok, LANES), lambda c: (0, c))],
-        out_specs=[pl.BlockSpec((2, per, BLK, LANES), lambda c: (c, 0, 0, 0))] * chunks,
-        out_shape=[shape] * chunks,
-        cost_estimate=pl.CostEstimate(flops=0, bytes_accessed=4 * tok * width, transcendentals=0),
+def pack_q(query, first_pair, per):
+    width = query.shape[1]
+    rows = per * 2 * BLK
+    row_block = first_pair // per
+
+    def body(q_ref, o_ref):
+        for p in range(per):
+            for c in range(width // LANES):
+                cols = slice(c * LANES, (c + 1) * LANES)
+                a = q_ref[2 * p * BLK : (2 * p + 1) * BLK, cols] * jnp.bfloat16(0.125)
+                b = q_ref[(2 * p + 1) * BLK : (2 * p + 2) * BLK, cols] * jnp.bfloat16(0.125)
+                o_ref[2 * c, p] = jnp.concatenate([a[:, :DH], b[:, :DH]], axis=1)
+                o_ref[2 * c + 1, p] = jnp.concatenate([a[:, DH:], b[:, DH:]], axis=1)
+
+    return pl.pallas_call(
+        body,
+        grid=(1,),
+        in_specs=[pl.BlockSpec((rows, width), lambda i: (row_block, 0))],
+        out_specs=pl.BlockSpec((width // DH, per, BLK, LANES), lambda i: (0, 0, 0, 0)),
+        out_shape=jax.ShapeDtypeStruct((width // DH, per, BLK, LANES), jnp.bfloat16),
+        cost_estimate=pl.CostEstimate(flops=0, bytes_accessed=4 * rows * width, transcendentals=0),
         name="pack_q",
     )(query)
 
@@ -80,7 +84,7 @@
             pl.BlockSpec(memory_space=pltpu.SMEM),
             pl.BlockSpec(memory_space=pl.ANY),
         ],
-        out_specs=pl.BlockSpec(memory_space=pl.ANY),
+        out_specs=pl.BlockSpec(memory_space=pltpu.VMEM),
         out_shape=jax.ShapeDtypeStruct((count,) + kv_blocks.shape[1:], jnp.bfloat16),
         scratch_shapes=[pltpu.SemaphoreType.DMA((count,))],
         cost_estimate=pl.CostEstimate(
@@ -190,25 +194,27 @@
     def body(o_ref, *rest):
         out_ref = rest[-1]
         for p in range(per):
-            even, odd = o_ref[0, p], o_ref[1, p]
-            out_ref[2 * p * BLK : (2 * p + 1) * BLK, :] = jnp.concatenate(
-                [even[:, :DH], odd[:, :DH]], axis=1
-            )
-            out_ref[(2 * p + 1) * BLK : (2 * p + 2) * BLK, :] = jnp.concatenate(
-                [even[:, DH:], odd[:, DH:]], axis=1
-            )
+            for c in range(heads // 2):
+                cols = slice(c * LANES, (c + 1) * LANES)
+                even, odd = o_ref[2 * c, p], o_ref[2 * c + 1, p]
+                out_ref[2 * p * BLK : (2 * p + 1) * BLK, cols] = jnp.concatenate(
+                    [even[:, :DH], odd[:, :DH]], axis=1
+                )
+                out_ref[(2 * p + 1) * BLK : (2 * p + 2) * BLK, cols] = jnp.concatenate(
+                    [even[:, DH:], odd[:, DH:]], axis=1
+                )
 
     row_block = first_pair // per
-    in_specs = [pl.BlockSpec((2, per, BLK, LANES), lambda c: (c, 0, 0, 0))]
+    in_specs = [pl.BlockSpec((heads, per, BLK, LANES), lambda i: (0, 0, 0, 0))]
     args = [o_pairs]
     if into is not None:
         in_specs.append(pl.BlockSpec(memory_space=pl.ANY))
         args.append(into)
     return pl.pallas_call(
         body,
-        grid=(width // LANES,),
+        grid=(1,),
         in_specs=in_specs,
-        out_specs=pl.BlockSpec((rows, LANES), lambda c: (row_block, c)),
+        out_specs=pl.BlockSpec((rows, width), lambda i: (row_block, 0)),
         out_shape=jax.ShapeDtypeStruct((tok, width), jnp.bfloat16),
         input_output_aliases={1: 0} if into is not None else {},
         cost_estimate=pl.CostEstimate(flops=0, bytes_accessed=4 * rows * width, transcendentals=0),
@@ -228,9 +234,10 @@
     per_source = tok // BLK
     count = sources * per_source
 
+    per = per_source // (2 * chunks)
+    q_send = [pack_q(query, per * c, per) for c in range(chunks)]
+    q_first = across(q_send[0], "head")
     kv_send = pack_kv(key, value)
-    kv_blocks = across(kv_send, "head").reshape(count, BLK, LANES)
-    q_send = pack_q(query, chunks)
 
     rows = pattern[0]
     owner, pos = rows // count, rows % count
@@ -239,18 +246,31 @@
     high = jnp.max(jnp.where(of_range, pos[None], 0), axis=(1, 2))
     wanted = jnp.stack([low, high], axis=1)
     slot = jnp.sum(jnp.where(of_range, (pos[None] != low[:, None, None]).astype(jnp.int32), 0), axis=0)
-    table_index = jnp.where(owner == own, pos, count + owner * PMOST + slot).reshape(-1)
-    asked = lax.all_gather(wanted, "ctx", axis=0)
-    asked = lax.dynamic_index_in_dim(asked, own, axis=1, keepdims=False).reshape(-1)
-
-    picked = pick_blocks(kv_blocks, asked)
+    far = count + owner * PMOST + slot
+    table_index = jnp.where(owner == own, pos, far).reshape(-1)
+
+    asked = wanted[own ^ jnp.arange(ranges, dtype=jnp.int32)]
+    bit = 1
+    while bit < ranges:
+        asked = asked.reshape(ranges // (2 * bit), 2, bit, PMOST)
+        moved = lax.ppermute(asked[:, 1], "ctx", [(i, i ^ bit) for i in range(ranges)])
+        asked = jnp.stack([asked[:, 0], moved], axis=1).reshape(ranges, PMOST)
+        bit *= 2
+
+    kv_send, asked, q_first = lax.optimization_barrier((kv_send, asked, q_first))
+    kv_blocks = across(kv_send, "head").reshape(count, BLK, LANES)
+    by_range = asked[own ^ jnp.arange(ranges, dtype=jnp.int32)]
+    picked = pick_blocks(kv_blocks, by_range.reshape(-1))
     remote = across(picked.reshape(ranges, PMOST * BLK, LANES), "ctx")
     remote = remote.reshape(ranges * PMOST, BLK, LANES)
 
     out = None
-    per = per_source // (2 * chunks)
     for c in range(chunks):
-        q_pairs = across(q_send[c], "head")
+        if c == 0:
+            q_pairs = q_first
+        else:
+            send, remote = lax.optimization_barrier((q_send[c], remote))
+            q_pairs = across(send, "head")
         o_pairs = attend(table_index, q_pairs, kv_blocks, remote, 2 * per * c, per_source)
         o_pairs = across(o_pairs, "head")
         out = unpack(o_pairs, tok, width, per * c, out)

time: 225 us -> 200 us (0.89)
  blocking collectives: 37.4 us -> 0 us
  Pallas kernels: 96.4 us -> 69.9 us
  waiting for transfers between devices: 54 us -> 79.1 us
  starting transfers between devices: 33.2 us -> 43.7 us
  local copies, waits for them, and re-layouts: 2.31 us -> 5.74 us
    all_gather x1 -> x0, blocking collectives: 25.2 us -> none  [on_device(): asked = lax.all_gather(wanted, 'ctx', axis=0)]
    all_to_all x5 -> x6, waiting for transfers between devices: 54 us -> 69.3 us  [across(): return lax.all_to_all(x, axis, split_axis=0, concat_axis=0, tiled=True)]
    pallas_call x1, Pallas kernels: 17.8 us -> 2.61 us  [pick_blocks(): pl.pallas_call(body, in_specs=[pl.BlockSpec(memory_space=pltpu.SMEM), pl....]
    all_to_all x1 -> x0, blocking collectives: 12.2 us -> none  [across(): return lax.all_to_all(x, axis, split_axis=0, concat_axis=0, tiled=True)]
    pallas_call x4 -> x5, Pallas kernels: 24.2 us -> 13 us  [the longest x2 5.25 us: pack_q(): pl.pallas_call(body, grid=(1,), in_specs=[pl.BlockSpec((rows, width), lam...]
    ppermute x0 -> x3, waiting for transfers between devices: none -> 9.82 us  [on_device(): lax.ppermute(asked[:, 1], 'ctx', [(i, i ^ bit) for i in range(ranges)])]
    ppermute x0 -> x3, starting transfers between devices: none -> 6.61 us  [on_device(): lax.ppermute(asked[:, 1], 'ctx', [(i, i ^ bit) for i in range(ranges)])]
    all_to_all x5 -> x6, starting transfers between devices: 33.2 us -> 37.1 us  [across(): return lax.all_to_all(x, axis, split_axis=0, concat_axis=0, tiled=True)]
  transfers between devices with their start and end apart: 5 -> 9, of which waited for: 2 -> 6; matrix products, arithmetic and copies ran while one was open for 1% -> 2% of each run, Pallas kernels for 37% -> 31%
where the time goes in v2:
time: 200 us; the launch traced here: 199 us
  waiting for transfers between devices  79.1 us (40%)
  Pallas kernels  69.9 us (35%)
  starting transfers between devices  43.7 us (22%)
  local copies, waits for them, and re-layouts  5.74 us (3%)
    all_to_all x6, waiting for transfers between devices, across(): return lax.all_to_all(x, axis, split_axis=0, concat_axis=0, tiled=True)  69.3 us
    pallas_call x2, Pallas kernels, attend(): pl.pallas_call(body, in_specs=[pl.BlockSpec(memory_space=pltpu.SMEM), pl....  54.3 us
    all_to_all x6, starting transfers between devices, across(): return lax.all_to_all(x, axis, split_axis=0, concat_axis=0, tiled=True)  37.1 us
    ppermute x3, waiting for transfers between devices, on_device(): lax.ppermute(asked[:, 1], 'ctx', [(i, i ^ bit) for i in range(ranges)])  9.82 us
    ppermute x3, starting transfers between devices, on_device(): lax.ppermute(asked[:, 1], 'ctx', [(i, i ^ bit) for i in range(ranges)])  6.61 us
    pallas_call x2, Pallas kernels, pack_q(): pl.pallas_call(body, grid=(1,), in_specs=[pl.BlockSpec((rows, width), lam...  5.25 us
    pallas_call x2, Pallas kernels, unpack(): pl.pallas_call(body, grid=(1,), in_specs=in_specs, out_specs=pl.BlockSpec...  5.14 us
  transfers between devices with their start and end apart: 9, of which 6 were waited for; matrix products, arithmetic and copies ran while one was open for 2% of the time, Pallas kernels for 31%

profile of v2, /device:TPU:1, one launch (start us, length us, event | category | flops | bytes accessed | tf_op | source)
XLA Modules:
  0.0 199.1 jit_solution(4648602557993452799)
XLA Ops:
  0.0 0.0 copy-start.3
  0.0 0.0 copy-start
  0.0 2.7 %pack_q.3 = bf16[16,2,128,128]{3,2,1,0:T(8,128)(2,1)} custom-call(bf16[1024,1024]{1,0:T(8,128)(2,1)} %q_ref.3), custom_call_target="tpu_custom_call" | custom-call | bytes 2097152 | tf_op jit(solution)/shard_map/pack_q/pallas_call | solution.py:58
  2.7 7.8 %all-to-all-start = ((bf16[16,2,128,128]{3,2,1,0:T(8,128)(2,1)}), bf16[16,2,128,128]{3,2,1,0:T(8,128)(2,1)S(1)}, u32[]{:S(2)}, u32[]{:S(2)}) async-start(bf16[16,2,128,128]{3,2,1,0:T(8,128)(2,1)} %pack_q.3), calls=%async_computation | async-start | bytes 2097152 | tf_op jit(solution)/shard_map/all_to_all | solution.py:226
  10.5 0.0 copy-done.3
  10.6 0.1 select_reduce_fusion.2
  10.8 0.2 select_reduce_fusion
  10.9 0.1 copy.39
  11.0 0.6 gather_fusion
  11.6 0.1 copy.52
  11.7 2.6 %collective-permute-start = (s32[4,1,2]{0,2,1:T(2,128)S(1)}, s32[4,1,2]{0,2,1:T(2,128)S(1)}, u32[]{:S(2)}, u32[]{:S(2)}) collective-permute-start(s32[4,1,2]{0,2,1:T(2,128)S(1)} %bitcast.44), channel_id=1, source_target_pairs={{0,16},{16,0},{32,48},{48,32},{64,80},{80,64},{96,112},{112,96},{1... | collective-permute-start | bytes 104 | tf_op jit(solution)/shard_map/ppermute | solution.py:256
  14.3 0.1 copy.53
  14.4 0.0 copy-done
  14.4 0.0 copy-start.1
  14.4 1.6 copy-done.1
  16.0 2.6 %pack_kv.1 = bf16[16,1024,128]{2,1,0:T(8,128)(2,1)} custom-call(bf16[1024,1024]{1,0:T(8,128)(2,1)S(1)} %copy-done, bf16[1024,1024]{1,0:T(8,128)(2,1)S(1)} %copy-done.1), custom_call_target="tpu_custom_call" | custom-call | bytes 8388608 | tf_op jit(solution)/shard_map/pack_kv/pallas_call | solution.py:32
  18.7 7.4 %collective-permute-done = s32[4,1,2]{0,2,1:T(2,128)S(1)} collective-permute-done((s32[4,1,2]{0,2,1:T(2,128)S(1)}, s32[4,1,2]{0,2,1:T(2,128)S(1)}, u32[]{:S(2)}, u32[]{:S(2)}) %collective-permute-start) | collective-permute-done | bytes 64 | tf_op jit(solution)/shard_map/ppermute | solution.py:256
  26.1 0.1 stack.33
  26.2 0.1 fusion.3
  26.3 0.1 copy.41
  26.4 1.2 collective-permute-start.1
  27.6 1.2 collective-permute-done.1
  28.8 0.1 copy.42
  28.9 0.1 pad_add_fusion
  29.0 0.1 copy.43
  29.1 0.1 reshape_reshape.4
  29.2 2.7 %collective-permute-start.2 = (s32[1,4,2]{1,2,0:T(2,128)S(1)}, s32[1,4,2]{1,2,0:T(2,128)S(1)}, u32[]{:S(2)}, u32[]{:S(2)}) collective-permute-start(s32[1,4,2]{1,2,0:T(2,128)S(1)} %get-tuple-element.24), channel_id=1, source_target_pairs={{0,64},{16,80},{32,96},{48,112},{64,0},{80,16},{96,32},{112,48},{1... | collective-permute-start | bytes 104 | tf_op jit(solution)/shard_map/ppermute | solution.py:256
  31.9 1.2 collective-permute-done.2
  33.1 0.1 reshape.54
  33.2 0.0 all-to-all-done
  33.2 7.3 %all-to-all-start.1 = ((bf16[16,1024,128]{2,1,0:T(8,128)(2,1)}), bf16[16,1024,128]{2,1,0:T(8,128)(2,1)}, u32[]{:S(2)}, u32[]{:S(2)}) async-start(bf16[16,1024,128]{2,1,0:T(8,128)(2,1)} %pack_kv.1), calls=%async_computation.1 | async-start | bytes 8388608 | tf_op jit(solution)/shard_map/all_to_all | solution.py:226
  40.5 0.1 copy.45
  40.6 0.6 gather_fusion.1
  41.2 0.6 reshape.55.w_ref
  41.7 48.5 %all-to-all-done.1 = bf16[16,1024,128]{2,1,0:T(8,128)(2,1)} async-done(((bf16[16,1024,128]{2,1,0:T(8,128)(2,1)}), bf16[16,1024,128]{2,1,0:T(8,128)(2,1)}, u32[]{:S(2)}, u32[]{:S(2)}) %all-to-all-start.1) | async-done | bytes 4194336 | tf_op jit(solution)/shard_map/all_to_all | solution.py:226
  90.2 2.6 %pick_blocks.1 = bf16[16,128,128]{2,1,0:T(8,128)(2,1)} custom-call(s32[16]{0:T(128)} %reshape.55.w_ref, bf16[128,128,128]{2,1,0:T(8,128)(2,1)} %bitcast.8.kv_ref.loc_ref), custom_call_target="tpu_custom_call" | custom-call | bytes 1048576 | tf_op jit(solution)/shard_map/pick_blocks/pallas_call | solution.py:81
  92.8 5.3 %all-to-all-start.2 = ((bf16[8,256,128]{2,1,0:T(8,128)(2,1)}), bf16[8,256,128]{2,1,0:T(8,128)(2,1)S(1)}, u32[]{:S(2)}, u32[]{:S(2)}) async-start(bf16[8,256,128]{2,1,0:T(8,128)(2,1)} %bitcast.36), calls=%async_computation.2 | async-start | bytes 1048576 | tf_op jit(solution)/shard_map/all_to_all | solution.py:226
  98.1 2.6 %pack_q.2 = bf16[16,2,128,128]{3,2,1,0:T(8,128)(2,1)} custom-call(bf16[1024,1024]{1,0:T(8,128)(2,1)} %q_ref.3), custom_call_target="tpu_custom_call" | custom-call | bytes 2097152 | tf_op jit(solution)/shard_map/pack_q/pallas_call | solution.py:58
  100.7 7.6 %all-to-all-done.2 = bf16[8,256,128]{2,1,0:T(8,128)(2,1)S(1)} async-done(((bf16[8,256,128]{2,1,0:T(8,128)(2,1)}), bf16[8,256,128]{2,1,0:T(8,128)(2,1)S(1)}, u32[]{:S(2)}, u32[]{:S(2)}) %all-to-all-start.2) | async-done | bytes 524320 | tf_op jit(solution)/shard_map/all_to_all | solution.py:226
  108.2 5.2 %all-to-all-start.3 = ((bf16[16,2,128,128]{3,2,1,0:T(8,128)(2,1)}), bf16[16,2,128,128]{3,2,1,0:T(8,128)(2,1)S(1)}, u32[]{:S(2)}, u32[]{:S(2)}) async-start(bf16[16,2,128,128]{3,2,1,0:T(8,128)(2,1)} %pack_q.2), calls=%async_computation.3 | async-start | bytes 2097152 | tf_op jit(solution)/shard_map/all_to_all | solution.py:226
  113.4 0.1 copy.37
  113.5 0.1 copy.38
  113.6 0.1 reduce_sum.12
  113.7 0.1 squeeze.12
  113.9 27.2 %attend.3 = bf16[32,128,128]{2,1,0:T(8,128)(2,1)} custom-call(s32[1536]{0:T(1024)S(1)} %fusion.idx_ref, bf16[32,128,128]{2,1,0:T(8,128)(2,1)S(1)} %bitcast.32, bf16[128,128,128]{2,1,0:T(8,128)(2,1)} %bitcast.8.kv_ref.loc_ref, bf16[16,128,128]{2,1,0:T(8,128)(2,1)S(1)} %bitcast.34), custom_call_target="tpu_custom_call" | custom-call | flops 6442450944 | bytes 6815744 | tf_op jit(solution)/shard_map/attend/pallas_call | solution.py:163
  141.0 0.0 all-to-all-done.3
  141.1 5.8 %all-to-all-start.5 = ((bf16[16,2,128,128]{3,2,1,0:T(8,128)(2,1)}), bf16[16,2,128,128]{3,2,1,0:T(8,128)(2,1)}, u32[]{:S(2)}, u32[]{:S(2)}) async-start(bf16[16,2,128,128]{3,2,1,0:T(8,128)(2,1)} %bitcast.14), calls=%async_computation.5 | async-start | bytes 2097152 | tf_op jit(solution)/shard_map/all_to_all | solution.py:226
  146.9 27.1 %attend.2 = bf16[32,128,128]{2,1,0:T(8,128)(2,1)} custom-call(s32[1536]{0:T(1024)S(1)} %fusion.idx_ref, bf16[32,128,128]{2,1,0:T(8,128)(2,1)S(1)} %bitcast.33, bf16[128,128,128]{2,1,0:T(8,128)(2,1)} %bitcast.8.kv_ref.loc_ref, bf16[16,128,128]{2,1,0:T(8,128)(2,1)S(1)} %bitcast.35), custom_call_target="tpu_custom_call" | custom-call | flops 6442450944 | bytes 6815744 | tf_op jit(solution)/shard_map/attend/pallas_call | solution.py:163
  174.0 0.0 all-to-all-done.5.o_ref
  174.0 5.7 %all-to-all-start.4 = ((bf16[16,2,128,128]{3,2,1,0:T(8,128)(2,1)}), bf16[16,2,128,128]{3,2,1,0:T(8,128)(2,1)S(1)}, u32[]{:S(2)}, u32[]{:S(2)}) async-start(bf16[16,2,128,128]{3,2,1,0:T(8,128)(2,1)} %bitcast.12), calls=%async_computation.4 | async-start | bytes 2097152 | tf_op jit(solution)/shard_map/all_to_all | solution.py:226
  179.7 2.6 %unpack.2.rest_0_ = bf16[1024,1024]{1,0:T(8,128)(2,1)} custom-call(bf16[16,2,128,128]{3,2,1,0:T(8,128)(2,1)} %all-to-all-done.5.o_ref), custom_call_target="tpu_custom_call" | custom-call | bytes 2097152 | tf_op jit(solution)/shard_map/unpack/pallas_call | solution.py:213
  182.3 13.3 %all-to-all-done.4.o_ref = bf16[16,2,128,128]{3,2,1,0:T(8,128)(2,1)S(1)} async-done(((bf16[16,2,128,128]{3,2,1,0:T(8,128)(2,1)}), bf16[16,2,128,128]{3,2,1,0:T(8,128)(2,1)S(1)}, u32[]{:S(2)}, u32[]{:S(2)}) %all-to-all-start.4) | async-done | bytes 1048608 | tf_op jit(solution)/shard_map/all_to_all | solution.py:226
  195.5 0.0 copy-start.2
  195.5 1.0 copy-done.2
  196.5 2.6 %unpack.3 = bf16[1024,1024]{1,0:T(8,128)(2,1)} custom-call(bf16[16,2,128,128]{3,2,1,0:T(8,128)(2,1)} %copy-done.2, bf16[1024,1024]{1,0:T(8,128)(2,1)} %unpack.2.rest_0_), custom_call_target="tpu_custom_call", output_to_operand_aliasing={{}: (1, {})} | custom-call | bytes 2097152 | tf_op jit(solution)/shard_map/unpack/pallas_call | solution.py:213
  (13 shorter events, 0.1 us)
Async XLA Ops:
  0.0 10.6 %copy-start.3 = (s32[1,128,12]{1,0,2:T(1,128)S(1)}, s32[1,128,12]{1,0,2:T(1,128)}, u32[]{:S(2)}) copy-start(s32[1,128,12]{1,0,2:T(1,128)} %param.7) | copy-start | bytes 18436
  0.0 14.4 %copy-start = (bf16[1024,1024]{1,0:T(8,128)(2,1)S(1)}, bf16[1024,1024]{1,0:T(8,128)(2,1)}, u32[]{:S(2)}) copy-start(bf16[1024,1024]{1,0:T(8,128)(2,1)} %k_ref.1) | copy-start | bytes 6291460
  2.7 30.5 %all-to-all-start = ((bf16[16,2,128,128]{3,2,1,0:T(8,128)(2,1)}), bf16[16,2,128,128]{3,2,1,0:T(8,128)(2,1)S(1)}, u32[]{:S(2)}, u32[]{:S(2)}) async-start(bf16[16,2,128,128]{3,2,1,0:T(8,128)(2,1)} %pack_q.3), calls=%async_computation | async-start | bytes 2097152 | tf_op jit(solution)/shard_map/all_to_all | solution.py:226
  11.7 14.4 %collective-permute-start = (s32[4,1,2]{0,2,1:T(2,128)S(1)}, s32[4,1,2]{0,2,1:T(2,128)S(1)}, u32[]{:S(2)}, u32[]{:S(2)}) collective-permute-start(s32[4,1,2]{0,2,1:T(2,128)S(1)} %bitcast.44), channel_id=1, source_target_pairs={{0,16},{16,0},{32,48},{48,32},{64,80},{80,64},{96,112},{112,96},{1... | collective-permute-start | bytes 104 | tf_op jit(solution)/shard_map/ppermute | solution.py:256
  14.4 1.6 copy-start.1
  26.4 2.4 %collective-permute-start.1 = (s32[2,2,2]{2,1,0:T(2,128)S(1)}, s32[2,2,2]{2,1,0:T(2,128)S(1)}, u32[]{:S(2)}, u32[]{:S(2)}) collective-permute-start(s32[2,2,2]{2,1,0:T(2,128)S(1)} %bitcast.41), channel_id=1, source_target_pairs={{0,32},{16,48},{32,0},{48,16},{64,96},{80,112},{96,64},{112,80},{1... | collective-permute-start | bytes 104 | tf_op jit(solution)/shard_map/ppermute | solution.py:256
  29.2 3.9 %collective-permute-start.2 = (s32[1,4,2]{1,2,0:T(2,128)S(1)}, s32[1,4,2]{1,2,0:T(2,128)S(1)}, u32[]{:S(2)}, u32[]{:S(2)}) collective-permute-start(s32[1,4,2]{1,2,0:T(2,128)S(1)} %get-tuple-element.24), channel_id=1, source_target_pairs={{0,64},{16,80},{32,96},{48,112},{64,0},{80,16},{96,32},{112,48},{1... | collective-permute-start | bytes 104 | tf_op jit(solution)/shard_map/ppermute | solution.py:256
  33.2 57.0 %all-to-all-start.1 = ((bf16[16,1024,128]{2,1,0:T(8,128)(2,1)}), bf16[16,1024,128]{2,1,0:T(8,128)(2,1)}, u32[]{:S(2)}, u32[]{:S(2)}) async-start(bf16[16,1024,128]{2,1,0:T(8,128)(2,1)} %pack_kv.1), calls=%async_computation.1 | async-start | bytes 8388608 | tf_op jit(solution)/shard_map/all_to_all | solution.py:226
  92.8 15.4 %all-to-all-start.2 = ((bf16[8,256,128]{2,1,0:T(8,128)(2,1)}), bf16[8,256,128]{2,1,0:T(8,128)(2,1)S(1)}, u32[]{:S(2)}, u32[]{:S(2)}) async-start(bf16[8,256,128]{2,1,0:T(8,128)(2,1)} %bitcast.36), calls=%async_computation.2 | async-start | bytes 1048576 | tf_op jit(solution)/shard_map/all_to_all | solution.py:226
  108.2 32.8 %all-to-all-start.3 = ((bf16[16,2,128,128]{3,2,1,0:T(8,128)(2,1)}), bf16[16,2,128,128]{3,2,1,0:T(8,128)(2,1)S(1)}, u32[]{:S(2)}, u32[]{:S(2)}) async-start(bf16[16,2,128,128]{3,2,1,0:T(8,128)(2,1)} %pack_q.2), calls=%async_computation.3 | async-start | bytes 2097152 | tf_op jit(solution)/shard_map/all_to_all | solution.py:226
  141.1 32.9 %all-to-all-start.5 = ((bf16[16,2,128,128]{3,2,1,0:T(8,128)(2,1)}), bf16[16,2,128,128]{3,2,1,0:T(8,128)(2,1)}, u32[]{:S(2)}, u32[]{:S(2)}) async-start(bf16[16,2,128,128]{3,2,1,0:T(8,128)(2,1)} %bitcast.14), calls=%async_computation.5 | async-start | bytes 2097152 | tf_op jit(solution)/shard_map/all_to_all | solution.py:226
  174.0 21.6 %all-to-all-start.4 = ((bf16[16,2,128,128]{3,2,1,0:T(8,128)(2,1)}), bf16[16,2,128,128]{3,2,1,0:T(8,128)(2,1)S(1)}, u32[]{:S(2)}, u32[]{:S(2)}) async-start(bf16[16,2,128,128]{3,2,1,0:T(8,128)(2,1)} %bitcast.12), calls=%async_computation.4 | async-start | bytes 2097152 | tf_op jit(solution)/shard_map/all_to_all | solution.py:226
  195.5 1.0 copy-start.2

commit v3 on v2

v3 whole, which is shorter than its diff:
```python
import jax
import jax.numpy as jnp
from jax import lax
from jax.experimental import pallas as pl
from jax.experimental.pallas import tpu as pltpu
from jax.sharding import PartitionSpec as P

DH = 64
BLK = 128
KPER = 12
PMOST = 2
LANES = 2 * DH
NT = (((1,), (1,)), ((), ()))
NN = (((1,), (0,)), ((), ()))
VMEM_LIMIT = 48 * 1024 * 1024
WHOLE_VMEM = 63 * 1024 * 1024


def put_q(q_ref, o_ref, row, pairs):
    for p in range(pairs):
        for c in range(q_ref.shape[1] // LANES):
            cols = slice(c * LANES, (c + 1) * LANES)
            rows = slice(row + p * BLK, row + (p + 1) * BLK)
            a = q_ref[2 * p * BLK : (2 * p + 1) * BLK, cols] * jnp.bfloat16(0.125)
            b = q_ref[(2 * p + 1) * BLK : (2 * p + 2) * BLK, cols] * jnp.bfloat16(0.125)
            o_ref[2 * c, rows] = jnp.concatenate([a[:, :DH], b[:, :DH]], axis=1)
            o_ref[2 * c + 1, rows] = jnp.concatenate([a[:, DH:], b[:, DH:]], axis=1)


def pack_first(key, value, query, steps, kv_per, q_per):
    width = key.shape[1]
    kv_rows = kv_per * BLK
    rows = (kv_per + q_per) * BLK

    def body(k_ref, v_ref, q_ref, o_ref):
        for c in range(width // LANES):
            k = k_ref[:, c * LANES : (c + 1) * LANES]
            v = v_ref[:, c * LANES : (c + 1) * LANES]
            o_ref[2 * c, :kv_rows] = jnp.concatenate([k[:, :DH], v[:, :DH]], axis=1)
            o_ref[2 * c + 1, :kv_rows] = jnp.concatenate([k[:, DH:], v[:, DH:]], axis=1)
        put_q(q_ref, o_ref, kv_rows, q_per)

    kv_spec = pl.BlockSpec((kv_rows, width), lambda i: (i, 0))
    return pl.pallas_call(
        body,
        grid=(steps,),
        in_specs=[kv_spec, kv_spec, pl.BlockSpec((2 * q_per * BLK, width), lambda i: (i, 0))],
        out_specs=pl.BlockSpec((width // DH, rows, LANES), lambda i: (0, i, 0)),
        out_shape=jax.ShapeDtypeStruct((width // DH, steps * rows, LANES), jnp.bfloat16),
        compiler_params=pltpu.CompilerParams(vmem_limit_bytes=WHOLE_VMEM),
        cost_estimate=pl.CostEstimate(
            flops=0, bytes_accessed=4 * steps * rows * width, transcendentals=0
        ),
        name="pack_first",
    )(key, value, query)


def pack_rest(query, row_block, pairs):
    width = query.shape[1]
    shape = (width // DH, pairs * BLK, LANES)

    def body(q_ref, o_ref):
        put_q(q_ref, o_ref, 0, pairs)

    return pl.pallas_call(
        body,
        grid=(1,),
        in_specs=[pl.BlockSpec((2 * pairs * BLK, width), lambda i: (row_block, 0))],
        out_specs=pl.BlockSpec(shape, lambda i: (0, 0, 0)),
        out_shape=jax.ShapeDtypeStruct(shape, jnp.bfloat16),
        compiler_params=pltpu.CompilerParams(vmem_limit_bytes=WHOLE_VMEM),
        cost_estimate=pl.CostEstimate(
            flops=0, bytes_accessed=4 * pairs * BLK * width, transcendentals=0
        ),
        name="pack_rest",
    )(query)


def pick_blocks(kv_blocks, wanted):
    count = wanted.shape[0]

    def body(w_ref, kv_ref, o_ref, sem):
        copies = [
            pltpu.make_async_copy(kv_ref.at[w_ref[i]], o_ref.at[i], sem.at[i]) for i in range(count)
        ]
        for c in copies:
            c.start()
        for c in copies:
            c.wait()

    return pl.pallas_call(
        body,
        in_specs=[
            pl.BlockSpec(memory_space=pltpu.SMEM),
            pl.BlockSpec(memory_space=pl.ANY),
        ],
        out_specs=pl.BlockSpec(memory_space=pltpu.VMEM),
        out_shape=jax.ShapeDtypeStruct((count,) + kv_blocks.shape[1:], jnp.bfloat16),
        scratch_shapes=[pltpu.SemaphoreType.DMA((count,))],
        cost_estimate=pl.CostEstimate(
            flops=0, bytes_accessed=count * BLK * LANES * 4, transcendentals=0
        ),
        name="pick_blocks",
    )(wanted, kv_blocks)


def attend(table_index, q_pairs, tables, sources, per, first_block, per_source, q_place):
    pairs = sources * per
    starts = [0]
    for t in tables:
        starts.append(starts[-1] + t.shape[0])
    extra = [] if q_pairs is None else [q_pairs]

    def body(idx_ref, *refs):
        q_refs, refs = refs[: len(extra)], refs[len(extra) :]
        t_refs, (o_ref, tab, s_buf, m_buf, sems) = refs[: len(tables)], refs[len(tables) :]
        copies = [
            pltpu.make_async_copy(r, tab.at[pl.ds(starts[i], starts[i + 1] - starts[i])], sems.at[i])
            for i, r in enumerate(t_refs)
        ]
        for c in copies:
            c.start()
        for c in copies:
            c.wait()
        zeros = jnp.zeros((BLK, DH), jnp.bfloat16)

        def entry(pair, half):
            block = (pair // per) * per_source + first_block + 2 * (pair % per) + half
            return block * KPER

        def keys_of(base, jj):
            return jnp.concatenate(
                [tab[idx_ref[base + 2 * jj]], tab[idx_ref[base + 2 * jj + 1]]], axis=0
            )

        def score(pair, half):
            base = entry(pair, half)
            lanes = slice(half * DH, (half + 1) * DH)
            q = q_refs[0][pair, :, lanes] if extra else tab[q_place(pair), :, lanes]
            q = jnp.concatenate([q, zeros], axis=1)
            top = None
            for jj in range(KPER // 2):
                s = lax.dot_general(q, keys_of(base, jj), NT, preferred_element_type=jnp.float32)
                s_buf[half, :, jj * 2 * BLK : (jj + 1) * 2 * BLK] = s
                both = jnp.maximum(s[:, :BLK], s[:, BLK:])
                top = both if top is None else jnp.maximum(top, both)
            m_buf[half] = jnp.broadcast_to(jnp.max(top, axis=1, keepdims=True), (BLK, LANES))

        def finish(pair, half):
            base = entry(pair, half)
            top = m_buf[half]
            top2 = jnp.concatenate([top, top], axis=1)
            total, acc = None, None
            for jj in range(KPER // 2):
                p = jnp.exp(s_buf[half, :, jj * 2 * BLK : (jj + 1) * 2 * BLK] - top2)
                both = p[:, :BLK] + p[:, BLK:]
                total = both if total is None else total + both
                part = lax.dot_general(
                    p.astype(jnp.bfloat16),
                    keys_of(base, jj),
                    NN,
                    preferred_element_type=jnp.float32,
                )
                acc = part if acc is None else acc + part
            total = jnp.sum(total, axis=1, keepdims=True)
            return (acc[:, DH:] / total).astype(jnp.bfloat16)

        score(0, 0)

        def step(i, carry):
            score(i, 1)
            a = finish(i, 0)
            score(jnp.minimum(i + 1, pairs - 1), 0)
            b = finish(i, 1)
            o_ref[i] = jnp.concatenate([a, b], axis=1)
            return carry

        lax.fori_loop(0, pairs, step, 0)

    return pl.pallas_call(
        body,
        in_specs=[pl.BlockSpec(memory_space=pltpu.SMEM)]
        + [pl.BlockSpec(memory_space=pltpu.VMEM)] * len(extra)
        + [pl.BlockSpec(memory_space=pl.ANY)] * len(tables),
        out_specs=pl.BlockSpec(memory_space=pltpu.VMEM),
        out_shape=jax.ShapeDtypeStruct((pairs, BLK, LANES), jnp.bfloat16),
        scratch_shapes=[
            pltpu.VMEM((starts[-1], BLK, LANES), jnp.bfloat16),
            pltpu.VMEM((2, BLK, KPER * BLK), jnp.float32),
            pltpu.VMEM((2, BLK, LANES), jnp.float32),
            pltpu.SemaphoreType.DMA((len(tables),)),
        ],
        compiler_params=pltpu.CompilerParams(vmem_limit_bytes=VMEM_LIMIT),
        cost_estimate=pl.CostEstimate(
            flops=pairs * 2 * KPER * BLK * BLK * LANES * 4,
            bytes_accessed=(starts[-1] + 2 * pairs) * BLK * LANES * 2,
            transcendentals=pairs * 2 * KPER * BLK * BLK,
        ),
        name="attend",
    )(table_index, *extra, *tables)


def unpack(o_pairs, tok, width, first_pair, into):
    heads, per = o_pairs.shape[:2]
    rows = per * 2 * BLK

    def body(o_any, *rest):
        out_ref, o_ref, result, sem = rest[-4:]
        loads = [
            pltpu.make_async_copy(o_any.at[:, p], o_ref.at[:, p], sem.at[p]) for p in range(per)
        ]
        for load in loads:
            load.start()
        stores = []
        for p in range(per):
            loads[p].wait()
            for c in range(heads // 2):
                cols = slice(c * LANES, (c + 1) * LANES)
                even, odd = o_ref[2 * c, p], o_ref[2 * c + 1, p]
                result[2 * p * BLK : (2 * p + 1) * BLK, cols] = jnp.concatenate(
                    [even[:, :DH], odd[:, :DH]], axis=1
                )
                result[(2 * p + 1) * BLK : (2 * p + 2) * BLK, cols] = jnp.concatenate(
                    [even[:, DH:], odd[:, DH:]], axis=1
                )
            part = pl.ds(2 * p * BLK, 2 * BLK)
            start = 2 * (first_pair + p) * BLK
            stores.append(
                pltpu.make_async_copy(
                    result.at[part], out_ref.at[pl.ds(start, 2 * BLK)], sem.at[per + p]
                )
            )
            stores[-1].start()
        for store in stores:
            store.wait()

    in_specs = [pl.BlockSpec(memory_space=pl.ANY)]
    args = [o_pairs]
    if into is not None:
        in_specs.append(pl.BlockSpec(memory_space=pl.ANY))
        args.append(into)
    return pl.pallas_call(
        body,
        in_specs=in_specs,
        out_specs=pl.BlockSpec(memory_space=pl.ANY),
        out_shape=jax.ShapeDtypeStruct((tok, width), jnp.bfloat16),
        scratch_shapes=[
            pltpu.VMEM(o_pairs.shape, jnp.bfloat16),
            pltpu.VMEM((rows, width), jnp.bfloat16),
            pltpu.SemaphoreType.DMA((2 * per,)),
        ],
        input_output_aliases={1: 0} if into is not None else {},
        cost_estimate=pl.CostEstimate(flops=0, bytes_accessed=4 * rows * width, transcendentals=0),
        name="unpack",
    )(*args)


def across(x, axis):
    return lax.all_to_all(x, axis, split_axis=0, concat_axis=0, tiled=True)


def on_device(query, key, value, pattern):
    tok, width = query.shape
    sources = lax.axis_size("head")
    ranges = lax.axis_size("ctx")
    own = lax.axis_index("ctx")
    per_source = tok // BLK
    count = sources * per_source

    half = per_source // 2
    per = half // 2
    steps = per
    kv_per = per_source // steps
    stride = kv_per + 1

    rows = pattern[0]
    owner, pos = rows // count, rows % count
    of_range = owner[None] == jnp.arange(ranges, dtype=jnp.int32)[:, None, None]
    low = jnp.min(jnp.where(of_range, pos[None], count - 1), axis=(1, 2))
    high = jnp.max(jnp.where(of_range, pos[None], 0), axis=(1, 2))
    wanted = jnp.stack([low, high], axis=1)
    slot = jnp.sum(jnp.where(of_range, (pos[None] != low[:, None, None]).astype(jnp.int32), 0), axis=0)
    first_far = sources * steps * stride

    def place(p):
        return p // kv_per * stride + p % kv_per

    table_index = jnp.where(owner == own, place(pos), first_far + owner * PMOST + slot).reshape(-1)

    asked = across(wanted, "ctx")
    send = pack_first(key, value, query, steps, kv_per, 1)
    send, asked = lax.optimization_barrier((send, asked))
    first = across(send, "head").reshape(-1, BLK, LANES)
    send_rest = pack_rest(query, 1, per)
    picked = pick_blocks(first, place(asked).reshape(-1))
    remote = across(picked.reshape(ranges, PMOST * BLK, LANES), "ctx")
    send_rest, remote = lax.optimization_barrier((send_rest, remote))
    tables = [first, remote.reshape(-1, BLK, LANES)]
    q_rest = across(send_rest, "head").reshape(-1, BLK, LANES)

    out = None
    for c in range(2):
        o_pairs = attend(
            table_index,
            None if c == 0 else q_rest,
            tables,
            sources,
            per,
            half * c,
            per_source,
            lambda pair: pair * stride + kv_per,
        )
        o_pairs = across(o_pairs.reshape(sources, per, BLK, LANES), "head")
        out = unpack(o_pairs, tok, width, per * c, out)
    return out


def solution(mesh):
    placed = (
        P(("ctx", "head"), None),
        P(("ctx", "head"), None),
        P(("ctx", "head"), None),
        P("head", "ctx", None),
    )
    return jax.shard_map(
        on_device,
        mesh=mesh,
        in_specs=placed,
        out_specs=P(("ctx", "head"), None),
        check_vma=False,
    )
```

time: 200 us -> 194 us (0.970)
  starting transfers between devices: 43.7 us -> 36.6 us
  waiting for transfers between devices: 79.1 us -> 82.9 us
  local copies, waits for them, and re-layouts: 5.74 us -> 2.82 us
    all_to_all x6, waiting for transfers between devices: 69.3 us -> 82.9 us  [across(): return lax.all_to_all(x, axis, split_axis=0, concat_axis=0, tiled=True)]
    ppermute x3 -> x0, waiting for transfers between devices: 9.82 us -> none  [on_device(): lax.ppermute(asked[:, 1], 'ctx', [(i, i ^ bit) for i in range(ranges)])]
    ppermute x3 -> x0, starting transfers between devices: 6.61 us -> none  [on_device(): lax.ppermute(asked[:, 1], 'ctx', [(i, i ^ bit) for i in range(ranges)])]
    pallas_call x7 -> x6, Pallas kernels: 67.3 us -> 66.9 us  [the longest x2 54.8 us: attend(): pl.pallas_call(body, in_specs=[pl.BlockSpec(memory_space=pltpu.SMEM)] + [...]
  transfers between devices with their start and end apart: 9 -> 6, of which waited for: 6 -> 4; matrix products, arithmetic and copies ran while one was open for 2% -> 1% of each run, Pallas kernels for 31% -> 33%
where the time goes in v3:
time: 194 us; the launch traced here: 193 us
  waiting for transfers between devices  82.9 us (43%)
  Pallas kernels  69.5 us (36%)
  starting transfers between devices  36.6 us (19%)
  local copies, waits for them, and re-layouts  2.82 us (1%)
    all_to_all x6, waiting for transfers between devices, across(): return lax.all_to_all(x, axis, split_axis=0, concat_axis=0, tiled=True)  82.9 us
    pallas_call x2, Pallas kernels, attend(): pl.pallas_call(body, in_specs=[pl.BlockSpec(memory_space=pltpu.SMEM)] + [...  54.8 us
    all_to_all x6, starting transfers between devices, across(): return lax.all_to_all(x, axis, split_axis=0, concat_axis=0, tiled=True)  36.6 us
    pallas_call x1, Pallas kernels, pack_first(): pl.pallas_call(body, grid=(steps,), in_specs=[kv_spec, kv_spec, pl.BlockS...  4.83 us
    pallas_call x2, Pallas kernels, unpack(): pl.pallas_call(body, in_specs=in_specs, out_specs=pl.BlockSpec(memory_spa...  4.62 us
  transfers between devices with their start and end apart: 6, of which 4 were waited for; matrix products, arithmetic and copies ran while one was open for 1% of the time, Pallas kernels for 33%

profile of v3, /device:TPU:1, one launch (start us, length us, event | category | flops | bytes accessed | tf_op | source)
XLA Modules:
  0.0 193.0 jit_solution(13115863271428104199)
XLA Ops:
  0.0 0.7 and_select_fusion.1
  0.8 0.1 select_reduce_fusion.2
  0.9 0.2 select_reduce_fusion
  1.1 0.7 copy.21
  1.7 7.5 %all-to-all-start = ((s32[8,1,2]{2,1,0:T(1,128)}), s32[8,1,2]{2,1,0:T(1,128)S(1)}, u32[]{:S(2)}, u32[]{:S(2)}) async-start(s32[8,1,2]{2,1,0:T(1,128)} %copy.21), calls=%async_computation | async-start | bytes 8192 | tf_op jit(solution)/shard_map/all_to_all | solution.py:259
  9.2 4.8 %pack_first.1 = bf16[16,1280,128]{2,1,0:T(8,128)(2,1)} custom-call(bf16[1024,1024]{1,0:T(8,128)(2,1)} %k_ref.1, bf16[1024,1024]{1,0:T(8,128)(2,1)} %v_ref.1, bf16[1024,1024]{1,0:T(8,128)(2,1)} %q_ref.3), custom_call_target="tpu_custom_call" | custom-call | bytes 5242880 | tf_op jit(solution)/shard_map/pack_first/pallas_call | solution.py:44
  14.0 1.6 all-to-all-done
  15.6 0.1 copy.22
  15.7 7.5 %all-to-all-start.1 = ((bf16[16,1280,128]{2,1,0:T(8,128)(2,1)}), bf16[16,1280,128]{2,1,0:T(8,128)(2,1)}, u32[]{:S(2)}, u32[]{:S(2)}) async-start(bf16[16,1280,128]{2,1,0:T(8,128)(2,1)} %pack_first.1), calls=%async_computation.1 | async-start | bytes 10485760 | tf_op jit(solution)/shard_map/all_to_all | solution.py:259
  23.3 0.1 copy.23
  23.4 0.6 reshape.27.w_ref
  24.0 60.2 %all-to-all-done.1 = bf16[16,1280,128]{2,1,0:T(8,128)(2,1)} async-done(((bf16[16,1280,128]{2,1,0:T(8,128)(2,1)}), bf16[16,1280,128]{2,1,0:T(8,128)(2,1)}, u32[]{:S(2)}, u32[]{:S(2)}) %all-to-all-start.1) | async-done | bytes 5242912 | tf_op jit(solution)/shard_map/all_to_all | solution.py:259
  84.2 2.7 %pick_blocks.1 = bf16[16,128,128]{2,1,0:T(8,128)(2,1)} custom-call(s32[16]{0:T(128)} %reshape.27.w_ref, bf16[160,128,128]{2,1,0:T(8,128)(2,1)} %bitcast.4.kv_ref.refs_1_.refs_0_), custom_call_target="tpu_custom_call" | custom-call | bytes 1048576 | tf_op jit(solution)/shard_map/pick_blocks/pallas_call | solution.py:91
  86.9 4.7 %all-to-all-start.2 = ((bf16[8,256,128]{2,1,0:T(8,128)(2,1)}), bf16[8,256,128]{2,1,0:T(8,128)(2,1)S(1)}, u32[]{:S(2)}, u32[]{:S(2)}) async-start(bf16[8,256,128]{2,1,0:T(8,128)(2,1)} %bitcast.18), calls=%async_computation.2 | async-start | bytes 1048576 | tf_op jit(solution)/shard_map/all_to_all | solution.py:259
  91.6 0.0 copy-start.1
  91.6 2.6 %pack_rest.1 = bf16[16,256,128]{2,1,0:T(8,128)(2,1)} custom-call(bf16[1024,1024]{1,0:T(8,128)(2,1)} %q_ref.3), custom_call_target="tpu_custom_call" | custom-call | bytes 1048576 | tf_op jit(solution)/shard_map/pack_rest/pallas_call | solution.py:65
  94.2 7.6 %all-to-all-done.2 = bf16[8,256,128]{2,1,0:T(8,128)(2,1)S(1)} async-done(((bf16[8,256,128]{2,1,0:T(8,128)(2,1)}), bf16[8,256,128]{2,1,0:T(8,128)(2,1)S(1)}, u32[]{:S(2)}, u32[]{:S(2)}) %all-to-all-start.2) | async-done | bytes 524320 | tf_op jit(solution)/shard_map/all_to_all | solution.py:259
  101.7 5.2 %all-to-all-start.3 = ((bf16[16,256,128]{2,1,0:T(8,128)(2,1)}), bf16[16,256,128]{2,1,0:T(8,128)(2,1)S(1)}, u32[]{:S(2)}, u32[]{:S(2)}) async-start(bf16[16,256,128]{2,1,0:T(8,128)(2,1)} %pack_rest.1), calls=%async_computation.3 | async-start | bytes 2097152 | tf_op jit(solution)/shard_map/all_to_all | solution.py:259
  106.9 0.0 copy-done.1
  106.9 0.1 copy.19
  107.0 0.1 copy.20
  107.1 0.1 reduce_sum.12
  107.2 0.1 squeeze.3
  107.4 27.5 %attend.3 = bf16[32,128,128]{2,1,0:T(8,128)(2,1)} custom-call(s32[1536]{0:T(1024)S(1)} %fusion.2.idx_ref, bf16[160,128,128]{2,1,0:T(8,128)(2,1)} %bitcast.4.kv_ref.refs_1_.refs_0_, bf16[16,128,128]{2,1,0:T(8,128)(2,1)S(1)} %bitcast.16), custom_call_target="tpu_custom_call" | custom-call | flops 6442450944 | bytes 7864320 | tf_op jit(solution)/shard_map/attend/pallas_call | solution.py:180
  134.9 0.0 all-to-all-done.3
  134.9 5.8 %all-to-all-start.5 = ((bf16[16,2,128,128]{3,2,1,0:T(8,128)(2,1)}), bf16[16,2,128,128]{3,2,1,0:T(8,128)(2,1)}, u32[]{:S(2)}, u32[]{:S(2)}) async-start(bf16[16,2,128,128]{3,2,1,0:T(8,128)(2,1)} %bitcast.9), calls=%async_computation.5 | async-start | bytes 2097152 | tf_op jit(solution)/shard_map/all_to_all | solution.py:259
  140.7 27.4 %attend.2 = bf16[32,128,128]{2,1,0:T(8,128)(2,1)} custom-call(s32[1536]{0:T(1024)S(1)} %fusion.2.idx_ref, bf16[32,128,128]{2,1,0:T(8,128)(2,1)S(1)} %bitcast.15, bf16[160,128,128]{2,1,0:T(8,128)(2,1)} %bitcast.4.kv_ref.refs_1_.refs_0_, bf16[16,128,128]{2,1,0:T(8,128)(2,1)S(1)} %bitcast.17), custom_call_target="tpu_custom_call" | custom-call | flops 6442450944 | bytes 7864320 | tf_op jit(solution)/shard_map/attend/pallas_call | solution.py:180
  168.0 0.0 all-to-all-done.5.o_any
  168.0 5.9 %all-to-all-start.4 = ((bf16[16,2,128,128]{3,2,1,0:T(8,128)(2,1)}), bf16[16,2,128,128]{3,2,1,0:T(8,128)(2,1)S(1)}, u32[]{:S(2)}, u32[]{:S(2)}) async-start(bf16[16,2,128,128]{3,2,1,0:T(8,128)(2,1)} %bitcast.8), calls=%async_computation.4 | async-start | bytes 2097152 | tf_op jit(solution)/shard_map/all_to_all | solution.py:259
  173.9 2.3 %unpack.2.rest_0_ = bf16[1024,1024]{1,0:T(8,128)(2,1)} custom-call(bf16[16,2,128,128]{3,2,1,0:T(8,128)(2,1)} %all-to-all-done.5.o_any), custom_call_target="tpu_custom_call" | custom-call | bytes 2097152 | tf_op jit(solution)/shard_map/unpack/pallas_call | solution.py:242
  176.2 13.5 %all-to-all-done.4.o_any = bf16[16,2,128,128]{3,2,1,0:T(8,128)(2,1)S(1)} async-done(((bf16[16,2,128,128]{3,2,1,0:T(8,128)(2,1)}), bf16[16,2,128,128]{3,2,1,0:T(8,128)(2,1)S(1)}, u32[]{:S(2)}, u32[]{:S(2)}) %all-to-all-start.4) | async-done | bytes 1048608 | tf_op jit(solution)/shard_map/all_to_all | solution.py:259
  189.8 0.0 copy-start
  189.8 1.0 copy-done
  190.7 2.3 %unpack.3 = bf16[1024,1024]{1,0:T(8,128)(2,1)} custom-call(bf16[16,2,128,128]{3,2,1,0:T(8,128)(2,1)} %copy-done, bf16[1024,1024]{1,0:T(8,128)(2,1)} %unpack.2.rest_0_), custom_call_target="tpu_custom_call", output_to_operand_aliasing={{}: (1, {})} | custom-call | bytes 2097152 | tf_op jit(solution)/shard_map/unpack/pallas_call | solution.py:242
  (5 shorter events, 0.1 us)
Async XLA Ops:
  1.7 13.9 %all-to-all-start = ((s32[8,1,2]{2,1,0:T(1,128)}), s32[8,1,2]{2,1,0:T(1,128)S(1)}, u32[]{:S(2)}, u32[]{:S(2)}) async-start(s32[8,1,2]{2,1,0:T(1,128)} %copy.21), calls=%async_computation | async-start | bytes 8192 | tf_op jit(solution)/shard_map/all_to_all | solution.py:259
  15.7 68.5 %all-to-all-start.1 = ((bf16[16,1280,128]{2,1,0:T(8,128)(2,1)}), bf16[16,1280,128]{2,1,0:T(8,128)(2,1)}, u32[]{:S(2)}, u32[]{:S(2)}) async-start(bf16[16,1280,128]{2,1,0:T(8,128)(2,1)} %pack_first.1), calls=%async_computation.1 | async-start | bytes 10485760 | tf_op jit(solution)/shard_map/all_to_all | solution.py:259
  86.9 14.9 %all-to-all-start.2 = ((bf16[8,256,128]{2,1,0:T(8,128)(2,1)}), bf16[8,256,128]{2,1,0:T(8,128)(2,1)S(1)}, u32[]{:S(2)}, u32[]{:S(2)}) async-start(bf16[8,256,128]{2,1,0:T(8,128)(2,1)} %bitcast.18), calls=%async_computation.2 | async-start | bytes 1048576 | tf_op jit(solution)/shard_map/all_to_all | solution.py:259
  91.6 15.3 %copy-start.1 = (s32[1,128,12]{1,0,2:T(1,128)S(1)}, s32[1,128,12]{1,0,2:T(1,128)}, u32[]{:S(2)}) copy-start(s32[1,128,12]{1,0,2:T(1,128)} %param.7) | copy-start | bytes 18436
  101.7 33.1 %all-to-all-start.3 = ((bf16[16,256,128]{2,1,0:T(8,128)(2,1)}), bf16[16,256,128]{2,1,0:T(8,128)(2,1)S(1)}, u32[]{:S(2)}, u32[]{:S(2)}) async-start(bf16[16,256,128]{2,1,0:T(8,128)(2,1)} %pack_rest.1), calls=%async_computation.3 | async-start | bytes 2097152 | tf_op jit(solution)/shard_map/all_to_all | solution.py:259
  134.9 33.2 %all-to-all-start.5 = ((bf16[16,2,128,128]{3,2,1,0:T(8,128)(2,1)}), bf16[16,2,128,128]{3,2,1,0:T(8,128)(2,1)}, u32[]{:S(2)}, u32[]{:S(2)}) async-start(bf16[16,2,128,128]{3,2,1,0:T(8,128)(2,1)} %bitcast.9), calls=%async_computation.5 | async-start | bytes 2097152 | tf_op jit(solution)/shard_map/all_to_all | solution.py:259
  168.0 21.7 %all-to-all-start.4 = ((bf16[16,2,128,128]{3,2,1,0:T(8,128)(2,1)}), bf16[16,2,128,128]{3,2,1,0:T(8,128)(2,1)S(1)}, u32[]{:S(2)}, u32[]{:S(2)}) async-start(bf16[16,2,128,128]{3,2,1,0:T(8,128)(2,1)} %bitcast.8), calls=%async_computation.4 | async-start | bytes 2097152 | tf_op jit(solution)/shard_map/all_to_all | solution.py:259
  189.8 1.0 copy-start

commit v4 on v3

--- a/solution.py
+++ b/solution.py
@@ -12,7 +12,8 @@
 LANES = 2 * DH
 NT = (((1,), (1,)), ((), ()))
 NN = (((1,), (0,)), ((), ()))
-VMEM_LIMIT = 48 * 1024 * 1024
+ATTEND_VMEM = 12 * 1024 * 1024
+SMALL_VMEM = 6 * 1024 * 1024
 WHOLE_VMEM = 63 * 1024 * 1024
 
 
@@ -68,7 +69,7 @@
         in_specs=[pl.BlockSpec((2 * pairs * BLK, width), lambda i: (row_block, 0))],
         out_specs=pl.BlockSpec(shape, lambda i: (0, 0, 0)),
         out_shape=jax.ShapeDtypeStruct(shape, jnp.bfloat16),
-        compiler_params=pltpu.CompilerParams(vmem_limit_bytes=WHOLE_VMEM),
+        compiler_params=pltpu.CompilerParams(vmem_limit_bytes=SMALL_VMEM),
         cost_estimate=pl.CostEstimate(
             flops=0, bytes_accessed=4 * pairs * BLK * width, transcendentals=0
         ),
@@ -97,6 +98,7 @@
         out_specs=pl.BlockSpec(memory_space=pltpu.VMEM),
         out_shape=jax.ShapeDtypeStruct((count,) + kv_blocks.shape[1:], jnp.bfloat16),
         scratch_shapes=[pltpu.SemaphoreType.DMA((count,))],
+        compiler_params=pltpu.CompilerParams(vmem_limit_bytes=SMALL_VMEM),
         cost_estimate=pl.CostEstimate(
             flops=0, bytes_accessed=count * BLK * LANES * 4, transcendentals=0
         ),
@@ -104,24 +106,65 @@
     )(wanted, kv_blocks)
 
 
-def attend(table_index, q_pairs, tables, sources, per, first_block, per_source, q_place):
+def take_queries(table, pairs):
+    def body(t_ref, o_ref, sem):
+        stride = t_ref.shape[0] // pairs
+        copies = [
+            pltpu.make_async_copy(t_ref.at[i * stride + stride - 1], o_ref.at[i], sem.at[i])
+            for i in range(pairs)
+        ]
+        for c in copies:
+            c.start()
+        for c in copies:
+            c.wait()
+
+    return pl.pallas_call(
+        body,
+        in_specs=[pl.BlockSpec(memory_space=pl.ANY)],
+        out_specs=pl.BlockSpec(memory_space=pltpu.VMEM),
+        out_shape=jax.ShapeDtypeStruct((pairs, BLK, LANES), jnp.bfloat16),
+        scratch_shapes=[pltpu.SemaphoreType.DMA((pairs,))],
+        compiler_params=pltpu.CompilerParams(vmem_limit_bytes=SMALL_VMEM),
+        cost_estimate=pl.CostEstimate(
+            flops=0, bytes_accessed=pairs * BLK * LANES * 4, transcendentals=0
+        ),
+        name="take_queries",
+    )(table)
+
+
+def put_remote(table, remote, pairs):
+    count = remote.shape[0]
+
+    def body(t_ref, r_ref, o_ref, sem):
+        stride = t_ref.shape[0] // pairs
+        copies = [
+            pltpu.make_async_copy(r_ref.at[i], o_ref.at[i * stride + stride - 1], sem.at[i])
+            for i in range(count)
+        ]
+        for c in copies:
+            c.start()
+        for c in copies:
+            c.wait()
+
+    return pl.pallas_call(
+        body,
+        in_specs=[pl.BlockSpec(memory_space=pl.ANY)] * 2,
+        out_specs=pl.BlockSpec(memory_space=pl.ANY),
+        out_shape=jax.ShapeDtypeStruct(table.shape, jnp.bfloat16),
+        scratch_shapes=[pltpu.SemaphoreType.DMA((count,))],
+        input_output_aliases={0: 0},
+        compiler_params=pltpu.CompilerParams(vmem_limit_bytes=SMALL_VMEM),
+        cost_estimate=pl.CostEstimate(
+            flops=0, bytes_accessed=count * BLK * LANES * 4, transcendentals=0
+        ),
+        name="put_remote",
+    )(table, remote)
+
+
+def attend(table_index, q_pairs, table, sources, per, first_block, per_source):
     pairs = sources * per
-    starts = [0]
-    for t in tables:
-        starts.append(starts[-1] + t.shape[0])
-    extra = [] if q_pairs is None else [q_pairs]
-
-    def body(idx_ref, *refs):
-        q_refs, refs = refs[: len(extra)], refs[len(extra) :]
-        t_refs, (o_ref, tab, s_buf, m_buf, sems) = refs[: len(tables)], refs[len(tables) :]
-        copies = [
-            pltpu.make_async_copy(r, tab.at[pl.ds(starts[i], starts[i + 1] - starts[i])], sems.at[i])
-            for i, r in enumerate(t_refs)
-        ]
-        for c in copies:
-            c.start()
-        for c in copies:
-            c.wait()
+
+    def body(idx_ref, q_ref, tab, o_ref, s_buf, m_buf):
         zeros = jnp.zeros((BLK, DH), jnp.bfloat16)
 
         def entry(pair, half):
@@ -136,8 +179,7 @@
         def score(pair, half):
             base = entry(pair, half)
             lanes = slice(half * DH, (half + 1) * DH)
-            q = q_refs[0][pair, :, lanes] if extra else tab[q_place(pair), :, lanes]
-            q = jnp.concatenate([q, zeros], axis=1)
+            q = jnp.concatenate([q_ref[pair, :, lanes], zeros], axis=1)
             top = None
             for jj in range(KPER // 2):
                 s = lax.dot_general(q, keys_of(base, jj), NT, preferred_element_type=jnp.float32)
@@ -179,25 +221,25 @@
 
     return pl.pallas_call(
         body,
-        in_specs=[pl.BlockSpec(memory_space=pltpu.SMEM)]
-        + [pl.BlockSpec(memory_space=pltpu.VMEM)] * len(extra)
-        + [pl.BlockSpec(memory_space=pl.ANY)] * len(tables),
+        in_specs=[
+            pl.BlockSpec(memory_space=pltpu.SMEM),
+            pl.BlockSpec(memory_space=pltpu.VMEM),
+            pl.BlockSpec(memory_space=pltpu.VMEM),
+        ],
         out_specs=pl.BlockSpec(memory_space=pltpu.VMEM),
         out_shape=jax.ShapeDtypeStruct((pairs, BLK, LANES), jnp.bfloat16),
         scratch_shapes=[
-            pltpu.VMEM((starts[-1], BLK, LANES), jnp.bfloat16),
             pltpu.VMEM((2, BLK, KPER * BLK), jnp.float32),
             pltpu.VMEM((2, BLK, LANES), jnp.float32),
-            pltpu.SemaphoreType.DMA((len(tables),)),
         ],
-        compiler_params=pltpu.CompilerParams(vmem_limit_bytes=VMEM_LIMIT),
+        compiler_params=pltpu.CompilerParams(vmem_limit_bytes=ATTEND_VMEM),
         cost_estimate=pl.CostEstimate(
             flops=pairs * 2 * KPER * BLK * BLK * LANES * 4,
-            bytes_accessed=(starts[-1] + 2 * pairs) * BLK * LANES * 2,
+            bytes_accessed=(table.shape[0] + 2 * pairs) * BLK * LANES * 2,
             transcendentals=pairs * 2 * KPER * BLK * BLK,
         ),
         name="attend",
-    )(table_index, *extra, *tables)
+    )(table_index, q_pairs, table)
 
 
 def unpack(o_pairs, tok, width, first_pair, into):
@@ -250,6 +292,7 @@
             pltpu.SemaphoreType.DMA((2 * per,)),
         ],
         input_output_aliases={1: 0} if into is not None else {},
+        compiler_params=pltpu.CompilerParams(vmem_limit_bytes=SMALL_VMEM),
         cost_estimate=pl.CostEstimate(flops=0, bytes_accessed=4 * rows * width, transcendentals=0),
         name="unpack",
     )(*args)
@@ -280,12 +323,12 @@
     high = jnp.max(jnp.where(of_range, pos[None], 0), axis=(1, 2))
     wanted = jnp.stack([low, high], axis=1)
     slot = jnp.sum(jnp.where(of_range, (pos[None] != low[:, None, None]).astype(jnp.int32), 0), axis=0)
-    first_far = sources * steps * stride
 
     def place(p):
         return p // kv_per * stride + p % kv_per
 
-    table_index = jnp.where(owner == own, place(pos), first_far + owner * PMOST + slot).reshape(-1)
+    far = (owner * PMOST + slot) * stride + kv_per
+    table_index = jnp.where(owner == own, place(pos), far).reshape(-1)
 
     asked = across(wanted, "ctx")
     send = pack_first(key, value, query, steps, kv_per, 1)
@@ -294,22 +337,14 @@
     send_rest = pack_rest(query, 1, per)
     picked = pick_blocks(first, place(asked).reshape(-1))
     remote = across(picked.reshape(ranges, PMOST * BLK, LANES), "ctx")
-    send_rest, remote = lax.optimization_barrier((send_rest, remote))
-    tables = [first, remote.reshape(-1, BLK, LANES)]
+    q_first = take_queries(first, sources * per)
+    send_rest, remote, q_first = lax.optimization_barrier((send_rest, remote, q_first))
+    table = put_remote(first, remote.reshape(-1, BLK, LANES), sources * per)
     q_rest = across(send_rest, "head").reshape(-1, BLK, LANES)
 
     out = None
-    for c in range(2):
-        o_pairs = attend(
-            table_index,
-            None if c == 0 else q_rest,
-            tables,
-            sources,
-            per,
-            half * c,
-            per_source,
-            lambda pair: pair * stride + kv_per,
-        )
+    for c, q_pairs in enumerate((q_first, q_rest)):
+        o_pairs = attend(table_index, q_pairs, table, sources, per, half * c, per_source)
         o_pairs = across(o_pairs.reshape(sources, per, BLK, LANES), "head")
         out = unpack(o_pairs, tok, width, per * c, out)
     return out

time: 194 us -> 191 us (0.985)
  Pallas kernels: 69.5 us -> 67.4 us
    pallas_call x2 -> x4, Pallas kernels: 54.8 us -> 56 us  [the longest x2 53.6 us: attend(): pl.pallas_call(body, in_specs=[pl.BlockSpec(memory_space=pltpu.SMEM), pl....]
  transfers between devices with their start and end apart: 6 -> 6, of which waited for: 4 -> 4; matrix products, arithmetic and copies ran while one was open for 1% -> 0% of each run, Pallas kernels for 33% -> 33%
where the time goes in v4:
time: 191 us
  waiting for transfers between devices  84.1 us (44%)
  Pallas kernels  67.4 us (35%)
  starting transfers between devices  36.5 us (19%)
    all_to_all x6, waiting for transfers between devices, across(): return lax.all_to_all(x, axis, split_axis=0, concat_axis=0, tiled=True)  84.1 us
    pallas_call x2, Pallas kernels, attend(): pl.pallas_call(body, in_specs=[pl.BlockSpec(memory_space=pltpu.SMEM), pl....  53.6 us
    all_to_all x6, starting transfers between devices, across(): return lax.all_to_all(x, axis, split_axis=0, concat_axis=0, tiled=True)  36.5 us
    pallas_call x1, Pallas kernels, pack_first(): pl.pallas_call(body, grid=(steps,), in_specs=[kv_spec, kv_spec, pl.BlockS...  4.83 us
  transfers between devices with their start and end apart: 6, of which 4 were waited for; matrix products, arithmetic and copies ran while one was open for 0% of the time, Pallas kernels for 33%

profile of v4, /device:TPU:1, one launch (start us, length us, event | category | flops | bytes accessed | tf_op | source)
XLA Modules:
  0.0 190.6 jit_solution(16991308164067488060)
XLA Ops:
  0.0 0.7 and_select_fusion.1
  0.8 0.1 select_reduce_fusion.2
  0.9 0.2 select_reduce_fusion
  1.1 0.7 copy.22
  1.7 7.5 %all-to-all-start = ((s32[8,1,2]{2,1,0:T(1,128)}), s32[8,1,2]{2,1,0:T(1,128)S(1)}, u32[]{:S(2)}, u32[]{:S(2)}) async-start(s32[8,1,2]{2,1,0:T(1,128)} %copy.22), calls=%async_computation | async-start | bytes 8192 | tf_op jit(solution)/shard_map/all_to_all | solution.py:302
  9.2 4.8 %pack_first.1 = bf16[16,1280,128]{2,1,0:T(8,128)(2,1)} custom-call(bf16[1024,1024]{1,0:T(8,128)(2,1)} %k_ref.1, bf16[1024,1024]{1,0:T(8,128)(2,1)} %v_ref.1, bf16[1024,1024]{1,0:T(8,128)(2,1)} %q_ref.3), custom_call_target="tpu_custom_call" | custom-call | bytes 5242880 | tf_op jit(solution)/shard_map/pack_first/pallas_call | solution.py:45
  14.0 1.6 all-to-all-done
  15.6 0.1 copy.23
  15.7 7.5 %all-to-all-start.1 = ((bf16[16,1280,128]{2,1,0:T(8,128)(2,1)}), bf16[16,1280,128]{2,1,0:T(8,128)(2,1)}, u32[]{:S(2)}, u32[]{:S(2)}) async-start(bf16[16,1280,128]{2,1,0:T(8,128)(2,1)} %pack_first.1), calls=%async_computation.1 | async-start | bytes 10485760 | tf_op jit(solution)/shard_map/all_to_all | solution.py:302
  23.3 0.1 copy.24
  23.4 0.1 reshape.27.w_ref
  23.5 60.7 %all-to-all-done.1 = bf16[16,1280,128]{2,1,0:T(8,128)(2,1)} async-done(((bf16[16,1280,128]{2,1,0:T(8,128)(2,1)}), bf16[16,1280,128]{2,1,0:T(8,128)(2,1)}, u32[]{:S(2)}, u32[]{:S(2)}) %all-to-all-start.1) | async-done | bytes 5242912 | tf_op jit(solution)/shard_map/all_to_all | solution.py:302
  84.2 0.0 copy-start
  84.2 2.6 %pick_blocks.1 = bf16[16,128,128]{2,1,0:T(8,128)(2,1)} custom-call(s32[16]{0:T(128)S(1)} %reshape.27.w_ref, bf16[160,128,128]{2,1,0:T(8,128)(2,1)} %bitcast.4.kv_ref.t_ref), custom_call_target="tpu_custom_call" | custom-call | bytes 1048576 | tf_op jit(solution)/shard_map/pick_blocks/pallas_call | solution.py:92
  86.8 4.8 %all-to-all-start.2 = ((bf16[8,256,128]{2,1,0:T(8,128)(2,1)}), bf16[8,256,128]{2,1,0:T(8,128)(2,1)S(1)}, u32[]{:S(2)}, u32[]{:S(2)}) async-start(bf16[8,256,128]{2,1,0:T(8,128)(2,1)} %bitcast.5), calls=%async_computation.2 | async-start | bytes 1048576 | tf_op jit(solution)/shard_map/all_to_all | solution.py:302
  91.6 0.0 copy-done
  91.6 1.3 pack_rest.1
  92.9 1.4 take_queries.1.q_ref
  94.4 0.0 copy-start.1
  94.4 7.3 %all-to-all-done.2 = bf16[8,256,128]{2,1,0:T(8,128)(2,1)S(1)} async-done(((bf16[8,256,128]{2,1,0:T(8,128)(2,1)}), bf16[8,256,128]{2,1,0:T(8,128)(2,1)S(1)}, u32[]{:S(2)}, u32[]{:S(2)}) %all-to-all-start.2) | async-done | bytes 524320 | tf_op jit(solution)/shard_map/all_to_all | solution.py:302
  101.7 5.2 %all-to-all-start.3 = ((bf16[16,256,128]{2,1,0:T(8,128)(2,1)}), bf16[16,256,128]{2,1,0:T(8,128)(2,1)S(1)}, u32[]{:S(2)}, u32[]{:S(2)}) async-start(bf16[16,256,128]{2,1,0:T(8,128)(2,1)} %pack_rest.1), calls=%async_computation.3 | async-start | bytes 2097152 | tf_op jit(solution)/shard_map/all_to_all | solution.py:302
  106.9 0.0 copy-done.1
  106.9 0.1 copy.20
  107.0 0.1 copy.21
  107.1 0.1 reduce_sum.12
  107.2 0.1 squeeze.3
  107.3 1.0 put_remote.1.tab
  108.3 26.8 %attend.3 = bf16[32,128,128]{2,1,0:T(8,128)(2,1)} custom-call(s32[1536]{0:T(1024)S(1)} %fusion.2.idx_ref, bf16[32,128,128]{2,1,0:T(8,128)(2,1)S(1)} %take_queries.1.q_ref, bf16[160,128,128]{2,1,0:T(8,128)(2,1)} %put_remote.1.tab), custom_call_target="tpu_custom_call" | custom-call | flops 6442450944 | bytes 7340032 | tf_op jit(solution)/shard_map/attend/pallas_call | solution.py:222
  135.1 0.0 all-to-all-done.3
  135.1 5.8 %all-to-all-start.5 = ((bf16[16,2,128,128]{3,2,1,0:T(8,128)(2,1)}), bf16[16,2,128,128]{3,2,1,0:T(8,128)(2,1)S(1)}, u32[]{:S(2)}, u32[]{:S(2)}) async-start(bf16[16,2,128,128]{3,2,1,0:T(8,128)(2,1)} %bitcast.9), calls=%async_computation.5 | async-start | bytes 2097152 | tf_op jit(solution)/shard_map/all_to_all | solution.py:302
  140.9 26.8 %attend.2 = bf16[32,128,128]{2,1,0:T(8,128)(2,1)} custom-call(s32[1536]{0:T(1024)S(1)} %fusion.2.idx_ref, bf16[32,128,128]{2,1,0:T(8,128)(2,1)S(1)} %bitcast.16, bf16[160,128,128]{2,1,0:T(8,128)(2,1)} %put_remote.1.tab), custom_call_target="tpu_custom_call" | custom-call | flops 6442450944 | bytes 7340032 | tf_op jit(solution)/shard_map/attend/pallas_call | solution.py:222
  167.7 0.0 all-to-all-done.5.o_any
  167.7 5.7 %all-to-all-start.4 = ((bf16[16,2,128,128]{3,2,1,0:T(8,128)(2,1)}), bf16[16,2,128,128]{3,2,1,0:T(8,128)(2,1)S(1)}, u32[]{:S(2)}, u32[]{:S(2)}) async-start(bf16[16,2,128,128]{3,2,1,0:T(8,128)(2,1)} %bitcast.8), calls=%async_computation.4 | async-start | bytes 2097152 | tf_op jit(solution)/shard_map/all_to_all | solution.py:302
  173.4 1.3 unpack.2.rest_0_
  174.8 14.5 %all-to-all-done.4.o_any = bf16[16,2,128,128]{3,2,1,0:T(8,128)(2,1)S(1)} async-done(((bf16[16,2,128,128]{3,2,1,0:T(8,128)(2,1)}), bf16[16,2,128,128]{3,2,1,0:T(8,128)(2,1)S(1)}, u32[]{:S(2)}, u32[]{:S(2)}) %all-to-all-start.4) | async-done | bytes 1048608 | tf_op jit(solution)/shard_map/all_to_all | solution.py:302
  189.2 1.3 unpack.3
  (5 shorter events, 0.1 us)
Async XLA Ops:
  1.7 13.9 %all-to-all-start = ((s32[8,1,2]{2,1,0:T(1,128)}), s32[8,1,2]{2,1,0:T(1,128)S(1)}, u32[]{:S(2)}, u32[]{:S(2)}) async-start(s32[8,1,2]{2,1,0:T(1,128)} %copy.22), calls=%async_computation | async-start | bytes 8192 | tf_op jit(solution)/shard_map/all_to_all | solution.py:302
  15.7 68.5 %all-to-all-start.1 = ((bf16[16,1280,128]{2,1,0:T(8,128)(2,1)}), bf16[16,1280,128]{2,1,0:T(8,128)(2,1)}, u32[]{:S(2)}, u32[]{:S(2)}) async-start(bf16[16,1280,128]{2,1,0:T(8,128)(2,1)} %pack_first.1), calls=%async_computation.1 | async-start | bytes 10485760 | tf_op jit(solution)/shard_map/all_to_all | solution.py:302
  84.2 7.4 %copy-start = (bf16[1024,1024]{1,0:T(8,128)(2,1)S(1)}, bf16[1024,1024]{1,0:T(8,128)(2,1)}, u32[]{:S(2)}) copy-start(bf16[1024,1024]{1,0:T(8,128)(2,1)} %q_ref.3) | copy-start | bytes 6291460
  86.8 14.9 %all-to-all-start.2 = ((bf16[8,256,128]{2,1,0:T(8,128)(2,1)}), bf16[8,256,128]{2,1,0:T(8,128)(2,1)S(1)}, u32[]{:S(2)}, u32[]{:S(2)}) async-start(bf16[8,256,128]{2,1,0:T(8,128)(2,1)} %bitcast.5), calls=%async_computation.2 | async-start | bytes 1048576 | tf_op jit(solution)/shard_map/all_to_all | solution.py:302
  94.4 12.5 %copy-start.1 = (s32[1,128,12]{1,0,2:T(1,128)S(1)}, s32[1,128,12]{1,0,2:T(1,128)}, u32[]{:S(2)}) copy-start(s32[1,128,12]{1,0,2:T(1,128)} %param.7) | copy-start | bytes 18436
  101.7 33.4 %all-to-all-start.3 = ((bf16[16,256,128]{2,1,0:T(8,128)(2,1)}), bf16[16,256,128]{2,1,0:T(8,128)(2,1)S(1)}, u32[]{:S(2)}, u32[]{:S(2)}) async-start(bf16[16,256,128]{2,1,0:T(8,128)(2,1)} %pack_rest.1), calls=%async_computation.3 | async-start | bytes 2097152 | tf_op jit(solution)/shard_map/all_to_all | solution.py:302
  135.1 32.5 %all-to-all-start.5 = ((bf16[16,2,128,128]{3,2,1,0:T(8,128)(2,1)}), bf16[16,2,128,128]{3,2,1,0:T(8,128)(2,1)S(1)}, u32[]{:S(2)}, u32[]{:S(2)}) async-start(bf16[16,2,128,128]{3,2,1,0:T(8,128)(2,1)} %bitcast.9), calls=%async_computation.5 | async-start | bytes 2097152 | tf_op jit(solution)/shard_map/all_to_all | solution.py:302
  167.7 21.6 %all-to-all-start.4 = ((bf16[16,2,128,128]{3,2,1,0:T(8,128)(2,1)}), bf16[16,2,128,128]{3,2,1,0:T(8,128)(2,1)S(1)}, u32[]{:S(2)}, u32[]{:S(2)}) async-start(bf16[16,2,128,128]{3,2,1,0:T(8,128)(2,1)} %bitcast.8), calls=%async_computation.4 | async-start | bytes 2097152 | tf_op jit(solution)/shard_map/all_to_all | solution.py:302

commit v5 on v4

--- a/solution.py
+++ b/solution.py
@@ -217,7 +217,7 @@
             o_ref[i] = jnp.concatenate([a, b], axis=1)
             return carry
 
-        lax.fori_loop(0, pairs, step, 0)
+        lax.fori_loop(0, pairs, step, 0, unroll=8)
 
     return pl.pallas_call(
         body,

time: 191 us -> 179 us (0.937)
  Pallas kernels: 67.4 us -> 54.5 us
    pallas_call x2, Pallas kernels: 53.6 us -> 40.7 us  [attend(): pl.pallas_call(body, in_specs=[pl.BlockSpec(memory_space=pltpu.SMEM), pl....]
  transfers between devices with their start and end apart: 6 -> 6, of which waited for: 4 -> 4; matrix products, arithmetic and copies ran while one was open for 0% -> 0% of each run, Pallas kernels for 33% -> 28%
where the time goes in v5:
time: 179 us; the launch traced here: 178 us
  waiting for transfers between devices  84.1 us (47%)
  Pallas kernels  54.5 us (30%)
  starting transfers between devices  36.5 us (20%)
    all_to_all x6, waiting for transfers between devices, across(): return lax.all_to_all(x, axis, split_axis=0, concat_axis=0, tiled=True)  84.1 us
    pallas_call x2, Pallas kernels, attend(): pl.pallas_call(body, in_specs=[pl.BlockSpec(memory_space=pltpu.SMEM), pl....  40.7 us
    all_to_all x6, starting transfers between devices, across(): return lax.all_to_all(x, axis, split_axis=0, concat_axis=0, tiled=True)  36.5 us
    pallas_call x1, Pallas kernels, pack_first(): pl.pallas_call(body, grid=(steps,), in_specs=[kv_spec, kv_spec, pl.BlockS...  4.83 us
  transfers between devices with their start and end apart: 6, of which 4 were waited for; matrix products, arithmetic and copies ran while one was open for 0% of the time, Pallas kernels for 28%

profile of v5, /device:TPU:1, one launch (start us, length us, event | category | flops | bytes accessed | tf_op | source)
XLA Modules:
  0.0 177.8 jit_solution(10096702665029491747)
XLA Ops:
  0.0 0.7 and_select_fusion.1
  0.8 0.1 select_reduce_fusion.2
  0.9 0.2 select_reduce_fusion
  1.1 0.7 copy.22
  1.7 7.5 %all-to-all-start = ((s32[8,1,2]{2,1,0:T(1,128)}), s32[8,1,2]{2,1,0:T(1,128)S(1)}, u32[]{:S(2)}, u32[]{:S(2)}) async-start(s32[8,1,2]{2,1,0:T(1,128)} %copy.22), calls=%async_computation | async-start | bytes 8192 | tf_op jit(solution)/shard_map/all_to_all | solution.py:302
  9.2 4.8 %pack_first.1 = bf16[16,1280,128]{2,1,0:T(8,128)(2,1)} custom-call(bf16[1024,1024]{1,0:T(8,128)(2,1)} %k_ref.1, bf16[1024,1024]{1,0:T(8,128)(2,1)} %v_ref.1, bf16[1024,1024]{1,0:T(8,128)(2,1)} %q_ref.3), custom_call_target="tpu_custom_call" | custom-call | bytes 5242880 | tf_op jit(solution)/shard_map/pack_first/pallas_call | solution.py:45
  14.0 1.6 all-to-all-done
  15.6 0.1 copy.23
  15.7 7.5 %all-to-all-start.1 = ((bf16[16,1280,128]{2,1,0:T(8,128)(2,1)}), bf16[16,1280,128]{2,1,0:T(8,128)(2,1)}, u32[]{:S(2)}, u32[]{:S(2)}) async-start(bf16[16,1280,128]{2,1,0:T(8,128)(2,1)} %pack_first.1), calls=%async_computation.1 | async-start | bytes 10485760 | tf_op jit(solution)/shard_map/all_to_all | solution.py:302
  23.3 0.1 copy.24
  23.4 0.1 reshape.27.w_ref
  23.5 60.7 %all-to-all-done.1 = bf16[16,1280,128]{2,1,0:T(8,128)(2,1)} async-done(((bf16[16,1280,128]{2,1,0:T(8,128)(2,1)}), bf16[16,1280,128]{2,1,0:T(8,128)(2,1)}, u32[]{:S(2)}, u32[]{:S(2)}) %all-to-all-start.1) | async-done | bytes 5242912 | tf_op jit(solution)/shard_map/all_to_all | solution.py:302
  84.2 0.0 copy-start
  84.2 2.6 %pick_blocks.1 = bf16[16,128,128]{2,1,0:T(8,128)(2,1)} custom-call(s32[16]{0:T(128)S(1)} %reshape.27.w_ref, bf16[160,128,128]{2,1,0:T(8,128)(2,1)} %bitcast.4.kv_ref.t_ref), custom_call_target="tpu_custom_call" | custom-call | bytes 1048576 | tf_op jit(solution)/shard_map/pick_blocks/pallas_call | solution.py:92
  86.8 4.8 %all-to-all-start.2 = ((bf16[8,256,128]{2,1,0:T(8,128)(2,1)}), bf16[8,256,128]{2,1,0:T(8,128)(2,1)S(1)}, u32[]{:S(2)}, u32[]{:S(2)}) async-start(bf16[8,256,128]{2,1,0:T(8,128)(2,1)} %bitcast.5), calls=%async_computation.2 | async-start | bytes 1048576 | tf_op jit(solution)/shard_map/all_to_all | solution.py:302
  91.6 0.0 copy-done
  91.6 1.3 pack_rest.1
  92.9 1.4 take_queries.1.q_ref
  94.4 0.0 copy-start.1
  94.4 7.3 %all-to-all-done.2 = bf16[8,256,128]{2,1,0:T(8,128)(2,1)S(1)} async-done(((bf16[8,256,128]{2,1,0:T(8,128)(2,1)}), bf16[8,256,128]{2,1,0:T(8,128)(2,1)S(1)}, u32[]{:S(2)}, u32[]{:S(2)}) %all-to-all-start.2) | async-done | bytes 524320 | tf_op jit(solution)/shard_map/all_to_all | solution.py:302
  101.7 5.2 %all-to-all-start.3 = ((bf16[16,256,128]{2,1,0:T(8,128)(2,1)}), bf16[16,256,128]{2,1,0:T(8,128)(2,1)S(1)}, u32[]{:S(2)}, u32[]{:S(2)}) async-start(bf16[16,256,128]{2,1,0:T(8,128)(2,1)} %pack_rest.1), calls=%async_computation.3 | async-start | bytes 2097152 | tf_op jit(solution)/shard_map/all_to_all | solution.py:302
  106.9 0.0 copy-done.1
  106.9 0.1 copy.20
  107.0 0.1 copy.21
  107.1 0.1 reduce_sum.12
  107.2 0.1 squeeze.3
  107.3 1.0 put_remote.1.tab
  108.3 20.3 %attend.3 = bf16[32,128,128]{2,1,0:T(8,128)(2,1)} custom-call(s32[1536]{0:T(1024)S(1)} %fusion.2.idx_ref, bf16[32,128,128]{2,1,0:T(8,128)(2,1)S(1)} %take_queries.1.q_ref, bf16[160,128,128]{2,1,0:T(8,128)(2,1)} %put_remote.1.tab), custom_call_target="tpu_custom_call" | custom-call | flops 6442450944 | bytes 7340032 | tf_op jit(solution)/shard_map/attend/pallas_call | solution.py:222
  128.6 0.0 all-to-all-done.3
  128.6 5.8 %all-to-all-start.5 = ((bf16[16,2,128,128]{3,2,1,0:T(8,128)(2,1)}), bf16[16,2,128,128]{3,2,1,0:T(8,128)(2,1)S(1)}, u32[]{:S(2)}, u32[]{:S(2)}) async-start(bf16[16,2,128,128]{3,2,1,0:T(8,128)(2,1)} %bitcast.9), calls=%async_computation.5 | async-start | bytes 2097152 | tf_op jit(solution)/shard_map/all_to_all | solution.py:302
  134.4 20.3 %attend.2 = bf16[32,128,128]{2,1,0:T(8,128)(2,1)} custom-call(s32[1536]{0:T(1024)S(1)} %fusion.2.idx_ref, bf16[32,128,128]{2,1,0:T(8,128)(2,1)S(1)} %bitcast.16, bf16[160,128,128]{2,1,0:T(8,128)(2,1)} %put_remote.1.tab), custom_call_target="tpu_custom_call" | custom-call | flops 6442450944 | bytes 7340032 | tf_op jit(solution)/shard_map/attend/pallas_call | solution.py:222
  154.8 0.0 all-to-all-done.5.o_any
  154.8 5.7 %all-to-all-start.4 = ((bf16[16,2,128,128]{3,2,1,0:T(8,128)(2,1)}), bf16[16,2,128,128]{3,2,1,0:T(8,128)(2,1)S(1)}, u32[]{:S(2)}, u32[]{:S(2)}) async-start(bf16[16,2,128,128]{3,2,1,0:T(8,128)(2,1)} %bitcast.8), calls=%async_computation.4 | async-start | bytes 2097152 | tf_op jit(solution)/shard_map/all_to_all | solution.py:302
  160.5 1.3 unpack.2.rest_0_
  161.8 14.5 %all-to-all-done.4.o_any = bf16[16,2,128,128]{3,2,1,0:T(8,128)(2,1)S(1)} async-done(((bf16[16,2,128,128]{3,2,1,0:T(8,128)(2,1)}), bf16[16,2,128,128]{3,2,1,0:T(8,128)(2,1)S(1)}, u32[]{:S(2)}, u32[]{:S(2)}) %all-to-all-start.4) | async-done | bytes 1048608 | tf_op jit(solution)/shard_map/all_to_all | solution.py:302
  176.3 1.3 unpack.3
  (5 shorter events, 0.1 us)
Async XLA Ops:
  1.7 13.9 %all-to-all-start = ((s32[8,1,2]{2,1,0:T(1,128)}), s32[8,1,2]{2,1,0:T(1,128)S(1)}, u32[]{:S(2)}, u32[]{:S(2)}) async-start(s32[8,1,2]{2,1,0:T(1,128)} %copy.22), calls=%async_computation | async-start | bytes 8192 | tf_op jit(solution)/shard_map/all_to_all | solution.py:302
  15.7 68.5 %all-to-all-start.1 = ((bf16[16,1280,128]{2,1,0:T(8,128)(2,1)}), bf16[16,1280,128]{2,1,0:T(8,128)(2,1)}, u32[]{:S(2)}, u32[]{:S(2)}) async-start(bf16[16,1280,128]{2,1,0:T(8,128)(2,1)} %pack_first.1), calls=%async_computation.1 | async-start | bytes 10485760 | tf_op jit(solution)/shard_map/all_to_all | solution.py:302
  84.2 7.4 %copy-start = (bf16[1024,1024]{1,0:T(8,128)(2,1)S(1)}, bf16[1024,1024]{1,0:T(8,128)(2,1)}, u32[]{:S(2)}) copy-start(bf16[1024,1024]{1,0:T(8,128)(2,1)} %q_ref.3) | copy-start | bytes 6291460
  86.8 14.9 %all-to-all-start.2 = ((bf16[8,256,128]{2,1,0:T(8,128)(2,1)}), bf16[8,256,128]{2,1,0:T(8,128)(2,1)S(1)}, u32[]{:S(2)}, u32[]{:S(2)}) async-start(bf16[8,256,128]{2,1,0:T(8,128)(2,1)} %bitcast.5), calls=%async_computation.2 | async-start | bytes 1048576 | tf_op jit(solution)/shard_map/all_to_all | solution.py:302
  94.4 12.5 %copy-start.1 = (s32[1,128,12]{1,0,2:T(1,128)S(1)}, s32[1,128,12]{1,0,2:T(1,128)}, u32[]{:S(2)}) copy-start(s32[1,128,12]{1,0,2:T(1,128)} %param.7) | copy-start | bytes 18436
  101.7 26.9 %all-to-all-start.3 = ((bf16[16,256,128]{2,1,0:T(8,128)(2,1)}), bf16[16,256,128]{2,1,0:T(8,128)(2,1)S(1)}, u32[]{:S(2)}, u32[]{:S(2)}) async-start(bf16[16,256,128]{2,1,0:T(8,128)(2,1)} %pack_rest.1), calls=%async_computation.3 | async-start | bytes 2097152 | tf_op jit(solution)/shard_map/all_to_all | solution.py:302
  128.6 26.1 %all-to-all-start.5 = ((bf16[16,2,128,128]{3,2,1,0:T(8,128)(2,1)}), bf16[16,2,128,128]{3,2,1,0:T(8,128)(2,1)S(1)}, u32[]{:S(2)}, u32[]{:S(2)}) async-start(bf16[16,2,128,128]{3,2,1,0:T(8,128)(2,1)} %bitcast.9), calls=%async_computation.5 | async-start | bytes 2097152 | tf_op jit(solution)/shard_map/all_to_all | solution.py:302
  154.8 21.5 %all-to-all-start.4 = ((bf16[16,2,128,128]{3,2,1,0:T(8,128)(2,1)}), bf16[16,2,128,128]{3,2,1,0:T(8,128)(2,1)S(1)}, u32[]{:S(2)}, u32[]{:S(2)}) async-start(bf16[16,2,128,128]{3,2,1,0:T(8,128)(2,1)} %bitcast.8), calls=%async_computation.4 | async-start | bytes 2097152 | tf_op jit(solution)/shard_map/all_to_all | solution.py:302

commit v6 on v5

--- a/solution.py
+++ b/solution.py
@@ -330,9 +330,15 @@
     far = (owner * PMOST + slot) * stride + kv_per
     table_index = jnp.where(owner == own, place(pos), far).reshape(-1)
 
-    asked = across(wanted, "ctx")
+    asked = wanted[own ^ jnp.arange(ranges, dtype=jnp.int32)]
+    bit = ranges // 2
+    while bit:
+        asked = asked.reshape(ranges // (2 * bit), 2, bit, PMOST)
+        moved = lax.ppermute(asked[:, 1], "ctx", [(i, i ^ bit) for i in range(ranges)])
+        asked = jnp.stack([asked[:, 0], moved], axis=1).reshape(ranges, PMOST)
+        bit //= 2
+    asked = asked[own ^ jnp.arange(ranges, dtype=jnp.int32)]
     send = pack_first(key, value, query, steps, kv_per, 1)
-    send, asked = lax.optimization_barrier((send, asked))
     first = across(send, "head").reshape(-1, BLK, LANES)
     send_rest = pack_rest(query, 1, per)
     picked = pick_blocks(first, place(asked).reshape(-1))

time: 179 us -> 170 us (0.950)
  waiting for transfers between devices: 84.1 us -> 74.5 us
    all_to_all x6 -> x5, waiting for transfers between devices: 84.1 us -> 21.8 us  [across(): return lax.all_to_all(x, axis, split_axis=0, concat_axis=0, tiled=True)]
    ppermute x0 -> x3, waiting for transfers between devices: none -> 52.7 us  [on_device(): lax.ppermute(asked[:, 1], 'ctx', [(i, i ^ bit) for i in range(ranges)])]
    ppermute x0 -> x3, starting transfers between devices: none -> 6.98 us  [on_device(): lax.ppermute(asked[:, 1], 'ctx', [(i, i ^ bit) for i in range(ranges)])]
    all_to_all x6 -> x5, starting transfers between devices: 36.5 us -> 29.8 us  [across(): return lax.all_to_all(x, axis, split_axis=0, concat_axis=0, tiled=True)]
  transfers between devices with their start and end apart: 6 -> 8, of which waited for: 4 -> 5; matrix products, arithmetic and copies ran while one was open for 0% -> 2% of each run, Pallas kernels for 28% -> 27%
where the time goes in v6:
time: 170 us; the launch traced here: 169 us
  waiting for transfers between devices  74.5 us (44%)
  Pallas kernels  54.5 us (32%)
  starting transfers between devices  36.7 us (22%)
  local copies, waits for them, and re-layouts  2.48 us (1%)
    ppermute x3, waiting for transfers between devices, on_device(): lax.ppermute(asked[:, 1], 'ctx', [(i, i ^ bit) for i in range(ranges)])  52.7 us
    pallas_call x2, Pallas kernels, attend(): pl.pallas_call(body, in_specs=[pl.BlockSpec(memory_space=pltpu.SMEM), pl....  40.7 us
    all_to_all x5, starting transfers between devices, across(): return lax.all_to_all(x, axis, split_axis=0, concat_axis=0, tiled=True)  29.8 us
    all_to_all x5, waiting for transfers between devices, across(): return lax.all_to_all(x, axis, split_axis=0, concat_axis=0, tiled=True)  21.8 us
    ppermute x3, starting transfers between devices, on_device(): lax.ppermute(asked[:, 1], 'ctx', [(i, i ^ bit) for i in range(ranges)])  6.98 us
    pallas_call x1, Pallas kernels, pack_first(): pl.pallas_call(body, grid=(steps,), in_specs=[kv_spec, kv_spec, pl.BlockS...  4.78 us
  transfers between devices with their start and end apart: 8, of which 5 were waited for; matrix products, arithmetic and copies ran while one was open for 2% of the time, Pallas kernels for 27%

profile of v6, /device:TPU:1, one launch (start us, length us, event | category | flops | bytes accessed | tf_op | source)
XLA Modules:
  0.0 168.9 jit_solution(14380069892941362582)
XLA Ops:
  0.0 4.8 %pack_first.1 = bf16[16,1280,128]{2,1,0:T(8,128)(2,1)} custom-call(bf16[1024,1024]{1,0:T(8,128)(2,1)} %k_ref.1, bf16[1024,1024]{1,0:T(8,128)(2,1)} %v_ref.1, bf16[1024,1024]{1,0:T(8,128)(2,1)} %q_ref.3), custom_call_target="tpu_custom_call" | custom-call | bytes 5242880 | tf_op jit(solution)/shard_map/pack_first/pallas_call | solution.py:45
  4.8 0.0 copy-start.1
  4.8 8.0 %all-to-all-start = ((bf16[16,1280,128]{2,1,0:T(8,128)(2,1)}), bf16[16,1280,128]{2,1,0:T(8,128)(2,1)}, u32[]{:S(2)}, u32[]{:S(2)}) async-start(bf16[16,1280,128]{2,1,0:T(8,128)(2,1)} %pack_first.1), calls=%async_computation | async-start | bytes 10485760 | tf_op jit(solution)/shard_map/all_to_all | solution.py:302
  12.8 0.0 copy-done.1
  12.8 0.1 select_reduce_fusion.2
  13.0 0.2 select_reduce_fusion
  13.1 0.1 copy.43
  13.2 0.6 gather_fusion
  13.8 0.1 copy.57
  13.9 2.7 %collective-permute-start = (s32[1,4,2]{1,2,0:T(2,128)S(1)}, s32[1,4,2]{1,2,0:T(2,128)S(1)}, u32[]{:S(2)}, u32[]{:S(2)}) collective-permute-start(s32[1,4,2]{1,2,0:T(2,128)S(1)} %bitcast.38), channel_id=1, source_target_pairs={{0,64},{16,80},{32,96},{48,112},{64,0},{80,16},{96,32},{112,48},{1... | collective-permute-start | bytes 104 | tf_op jit(solution)/shard_map/ppermute | solution.py:337
  16.6 0.1 copy.58
  16.7 1.1 collective-permute-done
  17.8 0.1 stack.33
  17.9 0.1 copy.45
  18.0 1.6 collective-permute-start.1
  19.6 1.4 collective-permute-done.1
  21.0 0.1 copy.46
  21.1 0.1 copy.47
  21.2 0.1 reshape_reshape.4
  21.3 2.6 %collective-permute-start.2 = (s32[4,1,2]{0,2,1:T(2,128)S(1)}, s32[4,1,2]{0,2,1:T(2,128)S(1)}, u32[]{:S(2)}, u32[]{:S(2)}) collective-permute-start(s32[4,1,2]{0,2,1:T(2,128)S(1)} %get-tuple-element.20), channel_id=1, source_target_pairs={{0,16},{16,0},{32,48},{48,32},{64,80},{80,64},{96,112},{112,96},{1... | collective-permute-start | bytes 104 | tf_op jit(solution)/shard_map/ppermute | solution.py:337
  23.9 50.2 %collective-permute-done.2 = s32[4,1,2]{0,2,1:T(2,128)S(1)} collective-permute-done((s32[4,1,2]{0,2,1:T(2,128)S(1)}, s32[4,1,2]{0,2,1:T(2,128)S(1)}, u32[]{:S(2)}, u32[]{:S(2)}) %collective-permute-start.2) | collective-permute-done | bytes 64 | tf_op jit(solution)/shard_map/ppermute | solution.py:337
  74.2 0.1 copy.52
  74.3 0.6 gather_fusion.1
  74.8 0.1 gather.10
  74.9 0.0 all-to-all-done
  74.9 0.0 copy-start
  74.9 2.6 %pick_blocks.1 = bf16[16,128,128]{2,1,0:T(8,128)(2,1)} custom-call(s32[16]{0:T(128)S(1)} %fusion.9.w_ref, bf16[160,128,128]{2,1,0:T(8,128)(2,1)} %bitcast.11.kv_ref.t_ref), custom_call_target="tpu_custom_call" | custom-call | bytes 1048576 | tf_op jit(solution)/shard_map/pick_blocks/pallas_call | solution.py:92
  77.5 5.1 %all-to-all-start.1 = ((bf16[8,256,128]{2,1,0:T(8,128)(2,1)}), bf16[8,256,128]{2,1,0:T(8,128)(2,1)S(1)}, u32[]{:S(2)}, u32[]{:S(2)}) async-start(bf16[8,256,128]{2,1,0:T(8,128)(2,1)} %bitcast.12), calls=%async_computation.1 | async-start | bytes 1048576 | tf_op jit(solution)/shard_map/all_to_all | solution.py:302
  82.7 0.0 copy-done
  82.7 1.3 pack_rest.1
  84.0 1.4 take_queries.1.q_ref
  85.4 7.3 %all-to-all-done.1 = bf16[8,256,128]{2,1,0:T(8,128)(2,1)S(1)} async-done(((bf16[8,256,128]{2,1,0:T(8,128)(2,1)}), bf16[8,256,128]{2,1,0:T(8,128)(2,1)S(1)}, u32[]{:S(2)}, u32[]{:S(2)}) %all-to-all-start.1) | async-done | bytes 524320 | tf_op jit(solution)/shard_map/all_to_all | solution.py:302
  92.8 5.2 %all-to-all-start.2 = ((bf16[16,256,128]{2,1,0:T(8,128)(2,1)}), bf16[16,256,128]{2,1,0:T(8,128)(2,1)S(1)}, u32[]{:S(2)}, u32[]{:S(2)}) async-start(bf16[16,256,128]{2,1,0:T(8,128)(2,1)} %pack_rest.1), calls=%async_computation.2 | async-start | bytes 2097152 | tf_op jit(solution)/shard_map/all_to_all | solution.py:302
  97.9 0.1 copy.41
  98.1 0.1 copy.42
  98.2 0.1 reduce_sum.12
  98.3 0.1 squeeze.12
  98.4 1.0 put_remote.1.tab
  99.4 20.3 %attend.3 = bf16[32,128,128]{2,1,0:T(8,128)(2,1)} custom-call(s32[1536]{0:T(1024)S(1)} %fusion.2.idx_ref, bf16[32,128,128]{2,1,0:T(8,128)(2,1)S(1)} %take_queries.1.q_ref, bf16[160,128,128]{2,1,0:T(8,128)(2,1)} %put_remote.1.tab), custom_call_target="tpu_custom_call" | custom-call | flops 6442450944 | bytes 7340032 | tf_op jit(solution)/shard_map/attend/pallas_call | solution.py:222
  119.7 0.0 all-to-all-done.2
  119.7 5.8 %all-to-all-start.4 = ((bf16[16,2,128,128]{3,2,1,0:T(8,128)(2,1)}), bf16[16,2,128,128]{3,2,1,0:T(8,128)(2,1)S(1)}, u32[]{:S(2)}, u32[]{:S(2)}) async-start(bf16[16,2,128,128]{3,2,1,0:T(8,128)(2,1)} %bitcast.16), calls=%async_computation.4 | async-start | bytes 2097152 | tf_op jit(solution)/shard_map/all_to_all | solution.py:302
  125.5 20.3 %attend.2 = bf16[32,128,128]{2,1,0:T(8,128)(2,1)} custom-call(s32[1536]{0:T(1024)S(1)} %fusion.2.idx_ref, bf16[32,128,128]{2,1,0:T(8,128)(2,1)S(1)} %bitcast.30, bf16[160,128,128]{2,1,0:T(8,128)(2,1)} %put_remote.1.tab), custom_call_target="tpu_custom_call" | custom-call | flops 6442450944 | bytes 7340032 | tf_op jit(solution)/shard_map/attend/pallas_call | solution.py:222
  145.9 0.0 all-to-all-done.4.o_any
  145.9 5.7 %all-to-all-start.3 = ((bf16[16,2,128,128]{3,2,1,0:T(8,128)(2,1)}), bf16[16,2,128,128]{3,2,1,0:T(8,128)(2,1)S(1)}, u32[]{:S(2)}, u32[]{:S(2)}) async-start(bf16[16,2,128,128]{3,2,1,0:T(8,128)(2,1)} %bitcast.15), calls=%async_computation.3 | async-start | bytes 2097152 | tf_op jit(solution)/shard_map/all_to_all | solution.py:302
  151.6 1.3 unpack.2.rest_0_
  152.9 14.5 %all-to-all-done.3.o_any = bf16[16,2,128,128]{3,2,1,0:T(8,128)(2,1)S(1)} async-done(((bf16[16,2,128,128]{3,2,1,0:T(8,128)(2,1)}), bf16[16,2,128,128]{3,2,1,0:T(8,128)(2,1)S(1)}, u32[]{:S(2)}, u32[]{:S(2)}) %all-to-all-start.3) | async-done | bytes 1048608 | tf_op jit(solution)/shard_map/all_to_all | solution.py:302
  167.4 1.3 unpack.3
  (13 shorter events, 0.1 us)
Async XLA Ops:
  4.8 8.0 %copy-start.1 = (s32[1,128,12]{1,0,2:T(1,128)S(1)}, s32[1,128,12]{1,0,2:T(1,128)}, u32[]{:S(2)}) copy-start(s32[1,128,12]{1,0,2:T(1,128)} %param.7) | copy-start | bytes 18436
  4.8 70.1 %all-to-all-start = ((bf16[16,1280,128]{2,1,0:T(8,128)(2,1)}), bf16[16,1280,128]{2,1,0:T(8,128)(2,1)}, u32[]{:S(2)}, u32[]{:S(2)}) async-start(bf16[16,1280,128]{2,1,0:T(8,128)(2,1)} %pack_first.1), calls=%async_computation | async-start | bytes 10485760 | tf_op jit(solution)/shard_map/all_to_all | solution.py:302
  13.9 3.9 %collective-permute-start = (s32[1,4,2]{1,2,0:T(2,128)S(1)}, s32[1,4,2]{1,2,0:T(2,128)S(1)}, u32[]{:S(2)}, u32[]{:S(2)}) collective-permute-start(s32[1,4,2]{1,2,0:T(2,128)S(1)} %bitcast.38), channel_id=1, source_target_pairs={{0,64},{16,80},{32,96},{48,112},{64,0},{80,16},{96,32},{112,48},{1... | collective-permute-start | bytes 104 | tf_op jit(solution)/shard_map/ppermute | solution.py:337
  18.0 3.0 %collective-permute-start.1 = (s32[2,2,2]{2,1,0:T(2,128)S(1)}, s32[2,2,2]{2,1,0:T(2,128)S(1)}, u32[]{:S(2)}, u32[]{:S(2)}) collective-permute-start(s32[2,2,2]{2,1,0:T(2,128)S(1)} %bitcast.35), channel_id=1, source_target_pairs={{0,32},{16,48},{32,0},{48,16},{64,96},{80,112},{96,64},{112,80},{1... | collective-permute-start | bytes 104 | tf_op jit(solution)/shard_map/ppermute | solution.py:337
  21.3 52.8 %collective-permute-start.2 = (s32[4,1,2]{0,2,1:T(2,128)S(1)}, s32[4,1,2]{0,2,1:T(2,128)S(1)}, u32[]{:S(2)}, u32[]{:S(2)}) collective-permute-start(s32[4,1,2]{0,2,1:T(2,128)S(1)} %get-tuple-element.20), channel_id=1, source_target_pairs={{0,16},{16,0},{32,48},{48,32},{64,80},{80,64},{96,112},{112,96},{1... | collective-permute-start | bytes 104 | tf_op jit(solution)/shard_map/ppermute | solution.py:337
  74.9 7.7 %copy-start = (bf16[1024,1024]{1,0:T(8,128)(2,1)S(1)}, bf16[1024,1024]{1,0:T(8,128)(2,1)}, u32[]{:S(2)}) copy-start(bf16[1024,1024]{1,0:T(8,128)(2,1)} %q_ref.3) | copy-start | bytes 6291460
  77.5 15.2 %all-to-all-start.1 = ((bf16[8,256,128]{2,1,0:T(8,128)(2,1)}), bf16[8,256,128]{2,1,0:T(8,128)(2,1)S(1)}, u32[]{:S(2)}, u32[]{:S(2)}) async-start(bf16[8,256,128]{2,1,0:T(8,128)(2,1)} %bitcast.12), calls=%async_computation.1 | async-start | bytes 1048576 | tf_op jit(solution)/shard_map/all_to_all | solution.py:302
  92.8 27.0 %all-to-all-start.2 = ((bf16[16,256,128]{2,1,0:T(8,128)(2,1)}), bf16[16,256,128]{2,1,0:T(8,128)(2,1)S(1)}, u32[]{:S(2)}, u32[]{:S(2)}) async-start(bf16[16,256,128]{2,1,0:T(8,128)(2,1)} %pack_rest.1), calls=%async_computation.2 | async-start | bytes 2097152 | tf_op jit(solution)/shard_map/all_to_all | solution.py:302
  119.7 26.1 %all-to-all-start.4 = ((bf16[16,2,128,128]{3,2,1,0:T(8,128)(2,1)}), bf16[16,2,128,128]{3,2,1,0:T(8,128)(2,1)S(1)}, u32[]{:S(2)}, u32[]{:S(2)}) async-start(bf16[16,2,128,128]{3,2,1,0:T(8,128)(2,1)} %bitcast.16), calls=%async_computation.4 | async-start | bytes 2097152 | tf_op jit(solution)/shard_map/all_to_all | solution.py:302
  145.9 21.6 %all-to-all-start.3 = ((bf16[16,2,128,128]{3,2,1,0:T(8,128)(2,1)}), bf16[16,2,128,128]{3,2,1,0:T(8,128)(2,1)S(1)}, u32[]{:S(2)}, u32[]{:S(2)}) async-start(bf16[16,2,128,128]{3,2,1,0:T(8,128)(2,1)} %bitcast.15), calls=%async_computation.3 | async-start | bytes 2097152 | tf_op jit(solution)/shard_map/all_to_all | solution.py:302
